TPU v7x, 32 devices: a whole 2x2x4 slice. The times are simulated.
32 devices in a mesh: group: 2 (over x), afd: 8 (over z, y), tensor: 2 (over core).
Axes of the slice: x: 2, y: 2, z: 4, core: 2. Of those that a mesh axis runs over, the one named last changes fastest.
Arguments:
- kv_cache: bfloat16 [896, 64, 576], P(('group', 'afd')), parts along dimension 0, may hold values from -6 to 6
- queries: bfloat16 [768, 64, 576], P(('group', 'afd'), 'tensor'), parts along dimension 0, may hold values from -64 to 64
- stream: bfloat16 [768, 7168], P('group', 'afd'), parts along dimension 0, may hold values from -3 to 3
- page_table: int32 [768, 8], P(('group', 'afd')), parts along dimension 0, may hold values from 0 to 55, as said below
- lengths: int32 [768], P(('group', 'afd')), parts along dimension 0, may hold values from 1 to 512, as said below
- send_pages: int32 [128, 2], P(('group', 'afd')), parts along dimension 0, may hold values from 40 to 55, as said below
- routes: int32 [768, 1], P('group'), parts along dimension 0, may hold values from 0 to 3; in each aligned block of 384 rows (0 to 383, 384 to 767, ...) at most 240 rows name the same one
- value_up: bfloat16 [64, 512, 128], P('tensor'), may hold values from -0.75 to 0.75
- output_weight: bfloat16 [8192, 7168], P('tensor', 'afd'), may hold values from -0.125 to 0.125
- norm_gain: float32 [7168], replicated, may hold values from 0.1 to 1.9
- gate_weight: bfloat16 [7168, 4096], P(None, ('afd', 'tensor')), may hold values from -0.0625 to 0.0625
- up_weight: bfloat16 [7168, 4096], P(None, ('afd', 'tensor')), may hold values from -0.0625 to 0.0625
- down_weight: bfloat16 [4096, 7168], P(('afd', 'tensor')), may hold values from -0.1875 to 0.1875
Outputs:
- mixed: bfloat16 [768, 7168], P('group', ('afd', 'tensor')), parts along dimension 0
There are 2 independent parts, one for each index of `group`. A program takes and returns all parts, laid end to end along the dimension named above; an argument that names none is the same for every part. Nothing has to cross between parts.
Inputs may be any that keep to these rules, and one draw needn't show every extreme that they name: `page_table`: row i lists the slots of request i on its device. The first ceil(lengths[i] / 64) entries are distinct and the later ones repeat the last of them; every slot of a device belongs to exactly one request. `lengths`: each device has a request of exactly 512 tokens. `send_pages`: row d of device b's block lists the 2 own pages that b sends to device d; each page of b from 40 up is listed exactly once. `routes`: at most 240 tokens name one expert, a bound that some block reaches.
All inputs are finite; a program needn't handle non-finite values.
Results may differ from a plain program's by a relative error of at most 0.007.
Values may be sent and summed in bfloat16 or wider, within the bound.
A program may use at most 192 MiB of HBM per device.

v0:
```python
import jax
import jax.numpy as jnp
from jax import lax
from jax.sharding import PartitionSpec as P

CAP = 240


score_scale = 0.07216878364870322
norm_eps = 1e-06


def score_block(queries, page_keys):
    return (
        jnp.einsum("rhc,rkc->rhk", queries, page_keys, preferred_element_type=jnp.float32)
        * score_scale
    )


def on_device(
    kv_cache,
    queries,
    stream,
    page_table,
    lengths,
    send_pages,
    routes,
    value_up,
    output_weight,
    norm_gain,
    gate_weight,
    up_weight,
    down_weight,
):
    afd_count = lax.axis_size("afd")
    tensor_index = lax.axis_index("tensor")
    pages_dev, page_len, channels = kv_cache.shape
    requests, max_pages = page_table.shape
    migrate_count = send_pages.shape[1]
    moved_total = afd_count * migrate_count
    local_count = pages_dev - moved_total
    latent = value_up.shape[1]
    span = max_pages * page_len
    outgoing = kv_cache[send_pages]
    arrived = lax.all_to_all(outgoing, "afd", split_axis=0, concat_axis=0, tiled=True)
    moved_pages = arrived.reshape(moved_total, page_len, channels)
    position = jnp.arange(span, dtype=jnp.int32)
    valid = position[None, None, :] < lengths[:, None, None]
    view = jnp.concatenate([kv_cache[:local_count], moved_pages], axis=0)
    page_keys = view[page_table].reshape(requests, span, channels)
    scores = score_block(queries, page_keys)
    scores = jnp.where(valid, scores, -jnp.inf)
    highest = jnp.max(scores, axis=-1, keepdims=True)
    exponent = jnp.exp(scores - highest)
    weights = (exponent / jnp.sum(exponent, axis=-1, keepdims=True)).astype(jnp.bfloat16)
    context = jnp.einsum(
        "rhk,rkl->rhl", weights, page_keys[:, :, :latent], preferred_element_type=jnp.float32
    ).astype(jnp.bfloat16)
    heads_out = jnp.einsum("rhl,hlv->rhv", context, value_up, preferred_element_type=jnp.float32)
    heads_out = heads_out.astype(jnp.bfloat16).reshape(requests, -1)
    partial_value = jnp.dot(
        lax.all_gather(heads_out, "afd", axis=0, tiled=True),
        output_weight,
        preferred_element_type=jnp.float32,
    )
    attended = lax.psum(partial_value, "tensor")
    hidden = (stream.astype(jnp.float32) + attended).astype(jnp.bfloat16)
    route = routes[:, 0]
    token_count = route.shape[0]
    experts = afd_count // 2
    expert_ids = jnp.arange(experts, dtype=jnp.int32)
    onehot = (route[:, None] == expert_ids[None, :]).astype(jnp.int32)
    rank = jnp.sum((jnp.cumsum(onehot, axis=0) - onehot) * onehot, axis=1)
    counts = jnp.sum(onehot, axis=0)
    starts = jnp.cumsum(counts) - counts
    order = jnp.argsort(route * token_count + jnp.arange(token_count, dtype=jnp.int32))
    seats = jnp.arange(CAP, dtype=jnp.int32)
    picked = starts[:, None] + seats[None, :]
    filled = seats[None, :] < counts[:, None]
    owner = jnp.where(filled, order[jnp.minimum(picked, token_count - 1)], token_count)
    padded = jnp.concatenate([hidden, jnp.zeros((1, hidden.shape[1]), jnp.bfloat16)], axis=0)
    buffer = padded[owner]
    doubled = jnp.repeat(buffer, 2, axis=0)
    token_rows = lax.all_to_all(doubled, "afd", split_axis=0, concat_axis=2, tiled=True)[0]
    rows_wide = token_rows.astype(jnp.float32)
    normed = rows_wide * lax.rsqrt(
        jnp.mean(rows_wide * rows_wide, axis=-1, keepdims=True) + norm_eps
    )
    normed = (normed * norm_gain).astype(jnp.bfloat16)
    gate = jnp.dot(normed, gate_weight, preferred_element_type=jnp.float32)
    up = jnp.dot(normed, up_weight, preferred_element_type=jnp.float32)
    activated = (jax.nn.silu(gate) * up).astype(jnp.bfloat16)
    partial_out = jnp.dot(activated, down_weight, preferred_element_type=jnp.float32)
    width = partial_out.shape[1]
    slice_width = width // (2 * afd_count)
    returned = lax.all_to_all(
        partial_out.reshape(1, CAP, width).astype(jnp.bfloat16),
        ("afd", "tensor"),
        split_axis=2,
        concat_axis=0,
        tiled=True,
    ).astype(jnp.float32)
    expert_out = jnp.sum(returned.reshape(experts, 4, CAP, slice_width), axis=1)
    ffn_rows = expert_out.reshape(experts * CAP, slice_width)[route * CAP + rank]
    residual_cols = lax.dynamic_slice_in_dim(hidden, tensor_index * slice_width, slice_width, 1)
    return (residual_cols.astype(jnp.float32) + ffn_rows).astype(jnp.bfloat16)


def solution(mesh):
    in_specs = (
        P(("group", "afd"), None, None),
        P(("group", "afd"), "tensor", None),
        P("group", "afd"),
        P(("group", "afd"), None),
        P(("group", "afd")),
        P(("group", "afd"), None),
        P("group", None),
        P("tensor", None, None),
        P("tensor", "afd"),
        P(),
        P(None, ("afd", "tensor")),
        P(None, ("afd", "tensor")),
        P(("afd", "tensor"), None),
    )
    out_specs = P("group", ("afd", "tensor"))
    return jax.shard_map(
        on_device, mesh=mesh, in_specs=in_specs, out_specs=out_specs, check_vma=False
    )
```

profile of v0, /device:TPU:13, one launch (start us, length us, event | category | flops | bytes accessed | tf_op | source)
XLA Modules:
  0.0 493.6 jit_solution(17641724927989933465)
XLA Ops:
  7.5 4.1 gather_fusion
  11.6 5.7 %all-to-all-start = ((bf16[8,2,64,576]{3,2,1,0:T(8,128)(2,1)}), bf16[8,2,64,576]{3,2,1,0:T(8,128)(2,1)S(1)}, u32[]{:S(2)}, u32[]{:S(2)}) async-start(bf16[8,2,64,576]{3,2,1,0:T(8,128)(2,1)} %bitcast.84), calls=%async_computation | async-start | bytes 2621440 | tf_op jit(solution)/shard_map/all_to_all | solution.py:45
  17.3 3.9 slice.12
  21.5 24.6 %all-to-all-done = bf16[8,2,64,576]{3,2,1,0:T(8,128)(2,1)S(1)} async-done(((bf16[8,2,64,576]{3,2,1,0:T(8,128)(2,1)}), bf16[8,2,64,576]{3,2,1,0:T(8,128)(2,1)S(1)}, u32[]{:S(2)}, u32[]{:S(2)}) %all-to-all-start) | async-done | bytes 1179680 | tf_op jit(solution)/shard_map/all_to_all | solution.py:45
  46.1 4.6 pad_maximum_fusion
  50.7 17.8 %gather_fusion.1 = bf16[384,64,576]{2,1,0:T(8,128)(2,1)} fusion(bf16[56,64,576]{2,1,0:T(8,128)(2,1)} %pad_maximum_fusion, s32[1024]{0:T(1024)S(1)} %pad_clamp_fusion.3), kind=kCustom, calls=%fused_computation.1 | custom fusion | bytes 56624640 | tf_op jit(solution)/shard_map/gather | solution.py:50
  68.5 15.9 %fusion.39 = (f32[48,32]{1,0:T(8,128)S(1)}, f32[48,32,512]{2,1,0:T(8,128)}) fusion(pred[48,512]{1,0:T(8,128)(4,1)S(1)} %iota_compare_fusion, bf16[48,512,576]{2,1,0:T(8,128)(2,1)} %bitcast.75, bf16[48,32,576]{2,1,0:T(8,128)(2,1)S(1)} %copy-done), kind=kOutput, calls=%fused_computation.71 | convolution fusion | flops 909115904 | bytes 33257472 | tf_op jit(solution)/shard_map/sub | solution.py:54
  84.5 11.6 %fusion.9 = bf16[48,32,512]{2,1,0:T(8,128)(2,1)S(1)} fusion(bf16[48,512,576]{2,1,0:T(8,128)(2,1)} %bitcast.76, f32[48,32,512]{2,1,0:T(8,128)} %get-tuple-element.10, f32[48,32]{1,0:T(8,128)S(1)} %get-tuple-element.9), kind=kOutput, calls=%fused_computation.21 | convolution fusion | flops 807665664 | bytes 29890560 | tf_op jit(solution)/shard_map/rhk,rkl->rhl/dot_general | solution.py:56
  100.9 58.1 %all-gather.2.cloned.1.call-done = bf16[384,4096]{1,0:T(8,128)(2,1)} async-done(((bf16[48,4096]{1,0:T(8,128)(2,1)}), bf16[384,4096]{1,0:T(8,128)(2,1)}) %all-gather.2.cloned.1.call-update) | async-done | bytes 3145744 | tf_op jit(solution)/shard_map/all_gather | solution.py:62
  159.0 8.5 %fusion.43 = f32[384,896]{1,0:T(8,128)} fusion(bf16[384,4096]{1,0:T(8,128)(2,1)} %all-gather.2.cloned.1.call-done, bf16[4096,896]{1,0:T(8,128)(2,1)} %param.21), kind=kOutput, calls=%fused_computation.74 | convolution fusion | flops 2818572288 | bytes 11862016 | tf_op jit(solution)/shard_map/dot_general | solution.py:61
  168.2 3.8 sort.17
  171.9 6.5 %gather_fusion.2 = s32[960]{0:T(1024)S(1)} fusion(s32[384]{0:T(512)S(1)} %get-tuple-element.6, s32[1024]{0:T(1024)S(1)} %pad_clamp_fusion.2), kind=kCustom, calls=%fused_computation.2 | custom fusion | bytes 11520 | tf_op jit(solution)/shard_map/gather | solution.py:80
  178.7 10.7 %all-reduce.3.cloned.1.call-done = f32[384,896]{1,0:T(8,128)} async-done(((f32[384,896]{1,0:T(8,128)}), f32[384,896]{1,0:T(8,128)}) %all-reduce.3.cloned.1.call-update) | async-done | bytes 1376272 | tf_op jit(solution)/shard_map/psum | solution.py:66
  191.0 5.2 %gather_fusion.3 = bf16[960,896]{1,0:T(8,128)(2,1)} fusion(bf16[385,896]{1,0:T(8,128)(2,1)S(1)} %concatenate.7, s32[1024]{0:T(1024)S(1)} %pad_clamp_fusion.1), kind=kCustom, calls=%fused_computation.3 | custom fusion | bytes 3444480 | tf_op jit(solution)/shard_map/gather | solution.py:82
  197.9 80.5 %all_to_all.23 = bf16[8,240,896]{2,1,0:T(8,128)(2,1)S(1)} all-to-all(bf16[8,240,896]{2,1,0:T(8,128)(2,1)S(1)} %bitcast.81), channel_id=1, replica_groups=mesh['group'=2,'afd'=8,'tensor'=2] {'afd'}, dimensions={0} | all-to-all | bytes 6881280 | tf_op jit(solution)/shard_map/all_to_all | solution.py:84
  283.7 10.7 %fusion.3 = bf16[1,240,7168]{2,1,0:T(8,128)(2,1)} fusion(bf16[256,7168]{1,0:T(8,128)(2,1)} %param.25, bf16[7168,256]{1,0:T(8,128)(2,1)} %param.24, f32[240,256]{1,0:T(8,128)S(1)} %fusion.38, f32[240,7168]{1,0:T(8,128)} %bitcast.73, f32[7168]{0:T(1024)S(1)} %copy-done.6, f32[240]{0:T(256)S(1)} %add_rsqrt_fusion), kind=kOutput, calls=%fused_computation.11 | convolution fusion | flops 1768857600 | bytes 17937344 | tf_op jit(solution)/shard_map/dot_general | solution.py:93
  294.4 16.3 %copy.30 = bf16[1,240,7168]{1,0,2:T(2,128)(2,1)} copy(bf16[1,240,7168]{2,1,0:T(8,128)(2,1)} %fusion.3) | data formatting | bytes 6881280 | tf_op jit(solution)/shard_map/convert_element_type | solution.py:97
  311.2 42.1 %reduce.9 = bf16[7168,240]{1,0:T(8,128)(2,1)} reduce(bf16[7168,1,240]{2,1,0:T(2,128)(2,1)} %bitcast.77, bf16[]{:T(256)} %broadcast.188), dimensions={1}, to_apply=%bitcast.53.reduce_sub_computation | reduce | bytes 6881282
  353.3 13.5 %reshape.258 = bf16[16,2,53760]{2,1,0:T(2,128)(2,1)} reshape(bf16[7168,240]{1,0:T(8,128)(2,1)} %reduce.9) | data formatting | bytes 6881280
  366.8 7.7 %all-to-all-start.2 = ((bf16[16,2,53760]{2,1,0:T(2,128)(2,1)}), bf16[16,2,53760]{2,1,0:T(2,128)(2,1)}, u32[]{:S(2)}, u32[]{:S(2)}) async-start(bf16[16,2,53760]{2,1,0:T(2,128)(2,1)} %reshape.258), calls=%async_computation.2 | async-start | bytes 6881280 | tf_op jit(solution)/shard_map/all_to_all | solution.py:96
  374.5 76.3 %all-to-all-done.2 = bf16[16,2,53760]{2,1,0:T(2,128)(2,1)} async-done(((bf16[16,2,53760]{2,1,0:T(2,128)(2,1)}), bf16[16,2,53760]{2,1,0:T(2,128)(2,1)}, u32[]{:S(2)}, u32[]{:S(2)}) %all-to-all-start.2) | async-done | bytes 3440672 | tf_op jit(solution)/shard_map/all_to_all | solution.py:96
  450.8 16.2 %reshape.259 = bf16[7168,1,240]{2,1,0:T(2,128)(2,1)} reshape(bf16[16,2,53760]{2,1,0:T(2,128)(2,1)} %all-to-all-done.2) | data formatting | bytes 6881280
  470.7 3.8 convert.6
  474.4 3.9 reduce_sum.50
  (69 shorter events, 28.0 us)
Async XLA Ops:
  6.5 62.0 %copy-start = (bf16[48,32,576]{2,1,0:T(8,128)(2,1)S(1)}, bf16[48,32,576]{2,1,0:T(8,128)(2,1)}, u32[]{:S(2)}) copy-start(bf16[48,32,576]{2,1,0:T(8,128)(2,1)} %param.14) | copy-start | bytes 5308420
  11.6 34.5 %all-to-all-start = ((bf16[8,2,64,576]{3,2,1,0:T(8,128)(2,1)}), bf16[8,2,64,576]{3,2,1,0:T(8,128)(2,1)S(1)}, u32[]{:S(2)}, u32[]{:S(2)}) async-start(bf16[8,2,64,576]{3,2,1,0:T(8,128)(2,1)} %bitcast.84), calls=%async_computation | async-start | bytes 2621440 | tf_op jit(solution)/shard_map/all_to_all | solution.py:45
  17.3 3.9 copy-start.8
  17.3 4.1 copy-start.9
  17.3 141.8 %all-gather.2.cloned.1.call-start = ((), (), s32[]{:S(2)}) async-start(), calls=%async_computation.3 | async-start | bytes 3538944 | tf_op jit(solution)/shard_map/all_gather | solution.py:62
  84.5 11.6 %copy-start.3 = (bf16[32,512,128]{2,1,0:T(8,128)(2,1)S(1)}, bf16[32,512,128]{2,1,0:T(8,128)(2,1)}, u32[]{:S(2)}) copy-start(bf16[32,512,128]{2,1,0:T(8,128)(2,1)} %param.20) | copy-start | bytes 12582916
  96.1 3.2 copy-start.7
  99.0 90.4 %all-reduce.3.cloned.1.call-start = ((), (), s32[]{:S(2)}) async-start(), calls=%async_computation.4 | async-start | bytes 2752512 | tf_op jit(solution)/shard_map/psum | solution.py:66
  167.6 21.8 %copy-start.5 = (bf16[384,896]{1,0:T(8,128)(2,1)S(1)}, bf16[384,896]{1,0:T(8,128)(2,1)}, u32[]{:S(2)}) copy-start(bf16[384,896]{1,0:T(8,128)(2,1)} %param.15) | copy-start | bytes 2064388
  278.9 3.7 copy-start.4
  279.7 2.8 copy-start.2
  279.8 2.8 copy-start.6
  366.8 84.0 %all-to-all-start.2 = ((bf16[16,2,53760]{2,1,0:T(2,128)(2,1)}), bf16[16,2,53760]{2,1,0:T(2,128)(2,1)}, u32[]{:S(2)}, u32[]{:S(2)}) async-start(bf16[16,2,53760]{2,1,0:T(2,128)(2,1)} %reshape.258), calls=%async_computation.2 | async-start | bytes 6881280 | tf_op jit(solution)/shard_map/all_to_all | solution.py:96
  480.2 6.6 %copy-start.1 = (bf16[48,32,576]{2,1,0:T(8,128)(2,1)S(1)}, bf16[48,32,576]{2,1,0:T(8,128)(2,1)}, u32[]{:S(2)}) copy-start(bf16[48,32,576]{2,1,0:T(8,128)(2,1)} %param.14) | copy-start | bytes 5308420
Sparse Core Ops, SparseCore 0:
  99.1 59.8 all-gather.1
  167.7 21.6 all-reduce.2
where the time goes:
time: 495 us; the launch traced here: 494 us
  waiting for transfers between devices  170 us (34%)
  local copies, waits for them, and re-layouts  101 us (20%)
  blocking collectives  80.5 us (16%)
  other arithmetic  64.7 us (13%)
  matrix products  50 us (10%)
  starting transfers between devices  13.6 us (3%)
  between operations  13.6 us (3%)
    all_to_all x1, blocking collectives, on_device(): lax.all_to_all(doubled, 'afd', split_axis=0, concat_axis=2, tiled=True)[0]  80.5 us
    all_to_all x1, waiting for transfers between devices, on_device(): lax.all_to_all(partial_out.reshape(1, CAP, width).astype(jnp.bfloat16), (...  76.3 us
    all_gather x1, waiting for transfers between devices, on_device(): lax.all_gather(heads_out, 'afd', axis=0, tiled=True)  58.1 us
    unnamed x4, other arithmetic  42.6 us
    unnamed x24, local copies, waits for them, and re-layouts  33.1 us
    all_to_all x1, waiting for transfers between devices, on_device(): lax.all_to_all(outgoing, 'afd', split_axis=0, concat_axis=0, tiled=True)  24.6 us
    gather x1, local copies, waits for them, and re-layouts, on_device(): page_keys = view[page_table].reshape(requests, span, channels)  17.8 us
    convert_element_type x1, local copies, waits for them, and re-layouts, on_device(): partial_out.reshape(1, CAP, width).astype(jnp.bfloat16)  16.3 us
  transfers between devices with their start and end apart: 4, of which 4 were waited for; matrix products, arithmetic and copies ran while one was open for 3% of the time, Pallas kernels for 0%

commit v1 on v0

v1 whole, which is shorter than its diff:
```python
import functools

import jax
import jax.numpy as jnp
from jax import lax
from jax.experimental import pallas as pl
from jax.experimental.pallas import tpu as pltpu
from jax.sharding import PartitionSpec as P

CAP = 240
MESH = pl.DeviceIdType.MESH
f32 = jnp.float32
bf16 = jnp.bfloat16

score_scale = 0.07216878364870322
norm_eps = 1e-06


def send(src, dst, send_sem, recv_sem, afd, tensor):
    return pltpu.make_async_remote_copy(
        src_ref=src,
        dst_ref=dst,
        send_sem=send_sem,
        recv_sem=recv_sem,
        device_id=(lax.axis_index("group"), afd, tensor),
        device_id_type=MESH,
    )


def greet(targets):
    barrier = pltpu.get_barrier_semaphore()
    for afd, tensor in targets:
        pl.semaphore_signal(
            barrier,
            inc=1,
            device_id=(lax.axis_index("group"), afd, tensor),
            device_id_type=MESH,
        )
    pl.semaphore_wait(barrier, len(targets))


def pages_kernel(count, out_ref, got_ref, sent_sem, got_sem, pass_sem, passed_sem, own_sem):
    me = lax.axis_index("afd")
    t = lax.axis_index("tensor")
    greet([(lax.rem(me + d, count), t) for d in range(1, count)] + [(me, 1 - t)])
    for d in range(1, count):
        to = lax.rem(me + d, count)
        send(out_ref.at[to], got_ref.at[me, t], sent_sem.at[to], got_sem.at[me], to, t).start()
    own = pltpu.make_async_copy(out_ref.at[me], got_ref.at[me, t], own_sem)
    own.start()
    own.wait()
    for d in range(count):
        src = lax.rem(me + count - d, count)
        if d > 0:
            send(out_ref.at[src], got_ref.at[src, t], sent_sem.at[src], got_sem.at[src], src, t).wait_recv()
        send(got_ref.at[src, t], got_ref.at[src, t], pass_sem.at[src], passed_sem.at[src], me, 1 - t).start()
    for d in range(count):
        src = lax.rem(me + count - d, count)
        back = send(got_ref.at[src, 1 - t], got_ref.at[src, 1 - t], pass_sem.at[src], passed_sem.at[src], me, 1 - t)
        back.wait_recv()
        back.wait_send()
    for d in range(1, count):
        to = lax.rem(me + d, count)
        send(out_ref.at[to], got_ref.at[me, t], sent_sem.at[to], got_sem.at[me], to, t).wait_send()


def exchange_pages(outgoing, count):
    dma = pltpu.SemaphoreType.DMA
    return pl.pallas_call(
        functools.partial(pages_kernel, count),
        out_shape=jax.ShapeDtypeStruct((count, 2) + outgoing.shape[1:], bf16),
        in_specs=[pl.BlockSpec(memory_space=pltpu.VMEM)],
        out_specs=pl.BlockSpec(memory_space=pltpu.VMEM),
        scratch_shapes=[dma((count,)), dma((count,)), dma((count,)), dma((count,)), dma],
        compiler_params=pltpu.CompilerParams(
            collective_id=0, has_side_effects=True, vmem_limit_bytes=40 * 2**20
        ),
    )(outgoing)


def project_kernel(
    pairs, heads_ref, w_hbm, stream_ref, hidden_ref,
    held, w, acc, half_out, half_in, w_sem, got_sem, up_sem, down_sem, side_sem, half_sems,
):
    me = lax.axis_index("afd")
    t = lax.axis_index("tensor")
    z, y = me // 2, lax.rem(me, 2)
    load = pltpu.make_async_copy(w_hbm, w, w_sem)
    load.start()
    greet(
        [(2 * lax.rem(z + d, pairs) + y, t) for d in range(1, pairs)]
        + [(2 * z + 1 - y, t), (me, 1 - t)]
    )
    held[me] = heads_ref[...]

    def side(slot):
        return send(held.at[slot], held.at[slot], side_sem.at[slot // 2], got_sem.at[slot], 2 * z + 1 - y, t)

    def up(slot):
        return send(held.at[slot], held.at[slot], up_sem.at[slot // 2], got_sem.at[slot], me + 2, t)

    def down(slot):
        return send(held.at[slot], held.at[slot], down_sem.at[slot // 2], got_sem.at[slot], me - 2, t)

    @pl.when(z + 1 < pairs)
    def _():
        up(me).start()

    @pl.when(z > 0)
    def _():
        down(me).start()

    side(me).start()
    for s in range(1, pairs):

        @pl.when(z - s >= 0)
        def _():
            slot = me - 2 * s
            up(slot).wait_recv()

            @pl.when(z + 1 < pairs)
            def _():
                up(slot).start()

            side(slot).start()

        @pl.when(z + s < pairs)
        def _():
            slot = me + 2 * s
            down(slot).wait_recv()

            @pl.when(z > 0)
            def _():
                down(slot).start()

            side(slot).start()

    for a in range(pairs):
        slot = 2 * a + 1 - y
        side(slot).wait_recv()
    for a in range(pairs):
        slot = 2 * a + y
        side(slot).wait_send()

        @pl.when((a <= z) & (z + 1 < pairs))
        def _():
            up(slot).wait_send()

        @pl.when((a >= z) & (z > 0))
        def _():
            down(slot).wait_send()

    load.wait()
    count, rows, depth = held.shape
    step = 512
    acc[...] = jnp.zeros_like(acc)

    def body(k, carry):
        at = pl.ds(pl.multiple_of(k * step, step), step)
        acc[...] += jnp.dot(
            held[:, :, at].reshape(count * rows, step), w[at, :], preferred_element_type=f32
        )
        return carry

    lax.fori_loop(0, depth // step, body, 0)
    width = half_out.shape[1]
    total = acc[...]
    left, right = total[:, :width], total[:, width:]
    first = t == 0
    half_out[...] = jnp.where(first, right, left)
    swap = send(half_out, half_in, half_sems.at[0], half_sems.at[1], me, 1 - t)
    swap.start()
    mine = jnp.where(first, left, right) + stream_ref[...].astype(f32)
    swap.wait()
    hidden_ref[...] = (mine + half_in[...]).astype(bf16)


def project(heads, weight, stream_half, pairs):
    dma = pltpu.SemaphoreType.DMA
    rows, depth = heads.shape
    tokens, width = stream_half.shape
    vmem = pl.BlockSpec(memory_space=pltpu.VMEM)
    return pl.pallas_call(
        functools.partial(project_kernel, pairs),
        out_shape=jax.ShapeDtypeStruct((tokens, width), bf16),
        in_specs=[vmem, pl.BlockSpec(memory_space=pl.ANY), vmem],
        out_specs=vmem,
        scratch_shapes=[
            pltpu.VMEM((2 * pairs, rows, depth), bf16),
            pltpu.VMEM(weight.shape, bf16),
            pltpu.VMEM((tokens, 2 * width), f32),
            pltpu.VMEM((tokens, width), f32),
            pltpu.VMEM((tokens, width), f32),
            dma,
            dma((2 * pairs,)),
            dma((pairs,)),
            dma((pairs,)),
            dma((pairs,)),
            dma((2,)),
        ],
        compiler_params=pltpu.CompilerParams(
            collective_id=1, has_side_effects=True, vmem_limit_bytes=48 * 2**20
        ),
    )(heads, weight, stream_half)


def experts_kernel(
    pairs, hidden_ref, pick_ref, place_ref, gain_ref, gate_hbm, up_hbm, down_hbm, out_ref,
    buf, rows, wg, wu, wd, acc_g, acc_u, squares, term1, send1, got1, send2, got2, send3, got3,
    w_sems, z_sem, row_sem, y_sem, t_sem, sems1, sems2, sems3,
):
    me = lax.axis_index("afd")
    t = lax.axis_index("tensor")
    z, y = me // 2, lax.rem(me, 2)
    beside = 2 * z + 1 - y
    width = hidden_ref.shape[1]
    loads = [
        pltpu.make_async_copy(a, b, w_sems.at[i])
        for i, (a, b) in enumerate(((gate_hbm, wg), (up_hbm, wu), (down_hbm, wd)))
    ]
    for load in loads:
        load.start()
    greet(
        [(2 * lax.rem(z + d, pairs) + y, t) for d in range(1, pairs)]
        + [(beside, t), (me, 1 - t)]
    )

    def along(e):
        return send(buf.at[e], rows.at[me, t], z_sem.at[e], row_sem.at[me, t], 2 * e + y, t)

    def across(slot):
        return send(rows.at[slot, t], rows.at[slot, t], y_sem.at[slot // 2], row_sem.at[slot, t], beside, t)

    def within(slot, side):
        return send(rows.at[slot, side], rows.at[slot, side], t_sem.at[slot], row_sem.at[slot, side], me, 1 - t)

    def build(d, carry):
        e = lax.rem(z + d, pairs)
        buf[e] = jnp.dot(pick_ref[e], hidden_ref[...], preferred_element_type=f32).astype(bf16)

        @pl.when(d < pairs)
        def _():
            along(e).start()

        return carry

    lax.fori_loop(1, pairs + 1, build, 0)
    rows[me, t] = buf[z]
    acc_g[...] = jnp.zeros_like(acc_g)
    acc_u[...] = jnp.zeros_like(acc_u)
    squares[...] = jnp.zeros_like(squares)
    loads[0].wait()
    loads[1].wait()

    def work(slot, side):
        block = slot * 2 + side
        wide = rows[slot, side].astype(f32)
        squares[...] += jnp.sum(wide * wide, axis=-1, keepdims=True)
        scaled = (wide * gain_ref[block]).astype(bf16)
        acc_g[...] += jnp.dot(scaled, wg[block], preferred_element_type=f32)
        acc_u[...] += jnp.dot(scaled, wu[block], preferred_element_type=f32)

    def straight(d, carry):
        slot = 2 * lax.rem(z + d, pairs) + y

        @pl.when(d > 0)
        def _():
            within(slot, t).wait_recv()

        across(slot).start()
        within(slot, t).start()
        work(slot, t)
        return carry

    lax.fori_loop(0, pairs, straight, 0)

    def sideways(d, carry):
        slot = 2 * lax.rem(z + d, pairs) + 1 - y
        within(slot, t).wait_recv()
        within(slot, t).start()
        work(slot, t)
        return carry

    lax.fori_loop(0, pairs, sideways, 0)

    def swapped(d, carry):
        for near in (True, False):
            slot = 2 * lax.rem(z + d, pairs) + (y if near else 1 - y)
            within(slot, 1 - t).wait_recv()
            work(slot, 1 - t)
        return carry

    lax.fori_loop(0, pairs, swapped, 0)
    depth = 2 * pairs * 2 * width
    scale = lax.rsqrt(squares[...] / depth + norm_eps)
    gate = acc_g[...] * scale
    activated = (jax.nn.silu(gate) * (acc_u[...] * scale)).astype(bf16)
    loads[2].wait()
    first = t == 0

    def swap1(a):
        return send(send1.at[a], got1.at[a], sems1.at[0, a], sems1.at[1, a], me, 1 - t)

    for a in range(2 * pairs):
        part = jnp.dot(
            activated, wd[:, a * 2 * width : (a + 1) * 2 * width], preferred_element_type=f32
        )
        left, right = part[:, :width], part[:, width:]
        send1[a] = jnp.where(first, right, left).astype(bf16)
        swap1(a).start()
        term1[a] = jnp.where(first, left, right)

    def swap2(e):
        return send(send2.at[e], got2.at[e], sems2.at[0, e], sems2.at[1, e], beside, t)

    def reduce2(d, carry):
        e = lax.rem(z + d, pairs)
        a = 2 * e + 1 - y
        swap1(a).wait_recv()
        send2[e] = (term1[a] + got1[a].astype(f32)).astype(bf16)
        swap2(e).start()
        return carry

    lax.fori_loop(1, pairs + 1, reduce2, 0)

    def give3(e):
        return send(send3.at[e], got3.at[z], sems3.at[0, e], sems3.at[1, z], 2 * e + y, t)

    def take3(e):
        return send(send3.at[e], got3.at[e], sems3.at[0, e], sems3.at[1, e], 2 * e + y, t)

    def reduce3(d, carry):
        e = lax.rem(z + d, pairs)
        a = 2 * e + y
        swap1(a).wait_recv()
        swap2(e).wait_recv()
        total = (term1[a] + got1[a].astype(f32) + got2[e].astype(f32)).astype(bf16)
        send3[e] = total

        @pl.when(d < pairs)
        def _():
            give3(e).start()

        return carry

    lax.fori_loop(1, pairs + 1, reduce3, 0)
    got3[z] = send3[z]
    mixed = hidden_ref[...].astype(f32)
    for d in range(pairs):
        e = lax.rem(z + d, pairs)
        if d > 0:
            take3(e).wait_recv()
        mixed += jnp.dot(place_ref[e], got3[e], preferred_element_type=f32)
    out_ref[...] = mixed.astype(bf16)
    for d in range(1, pairs):
        e = lax.rem(z + d, pairs)
        along(e).wait_send()
        give3(e).wait_send()
    for e in range(pairs):
        across(2 * e + y).wait_send()
        swap2(e).wait_send()
    for a in range(2 * pairs):
        within(a, t).wait_send()
        swap1(a).wait_send()


def run_experts(hidden, pick, place, gain, gate, up, down, pairs):
    dma = pltpu.SemaphoreType.DMA
    tokens, width = hidden.shape
    vmem = pl.BlockSpec(memory_space=pltpu.VMEM)
    hbm = pl.BlockSpec(memory_space=pl.ANY)
    count = 2 * pairs
    units = gate.shape[1]
    blocks = (2 * count, width, units)

    def tile(*lead):
        return pltpu.VMEM(lead + (CAP, width), bf16)

    return pl.pallas_call(
        functools.partial(experts_kernel, pairs),
        out_shape=jax.ShapeDtypeStruct((tokens, width), bf16),
        in_specs=[vmem, vmem, vmem, vmem, hbm, hbm, hbm],
        out_specs=vmem,
        scratch_shapes=[
            tile(pairs),
            tile(count, 2),
            pltpu.VMEM(blocks, bf16),
            pltpu.VMEM(blocks, bf16),
            pltpu.VMEM(down.shape, bf16),
            pltpu.VMEM((CAP, units), f32),
            pltpu.VMEM((CAP, units), f32),
            pltpu.VMEM((CAP, 1), f32),
            pltpu.VMEM((count, CAP, width), f32),
            tile(count),
            tile(count),
            tile(pairs),
            tile(pairs),
            tile(pairs),
            tile(pairs),
            dma((3,)),
            dma((pairs,)),
            dma((count, 2)),
            dma((pairs,)),
            dma((count,)),
            dma((2, count)),
            dma((2, pairs)),
            dma((2, pairs)),
        ],
        compiler_params=pltpu.CompilerParams(
            collective_id=2, has_side_effects=True, vmem_limit_bytes=56 * 2**20
        ),
    )(
        hidden, pick, place, gain.reshape(2 * count, 1, width),
        gate.reshape(blocks), up.reshape(blocks), down,
    )


def on_device(
    kv_cache,
    queries,
    stream,
    page_table,
    lengths,
    send_pages,
    routes,
    value_up,
    output_weight,
    norm_gain,
    gate_weight,
    up_weight,
    down_weight,
):
    afd_count = lax.axis_size("afd")
    pairs = afd_count // 2
    t = lax.axis_index("tensor")
    pages_dev, page_len, channels = kv_cache.shape
    requests, max_pages = page_table.shape
    migrate_count = send_pages.shape[1]
    moved_total = afd_count * migrate_count
    local_count = pages_dev - moved_total
    latent = value_up.shape[1]
    each = migrate_count // 2

    mine = lax.dynamic_slice_in_dim(send_pages, t * each, each, 1)
    moved = exchange_pages(kv_cache[mine], afd_count).reshape(moved_total, page_len, channels)

    slots = jnp.arange(pages_dev, dtype=jnp.int32)
    place = jnp.arange(max_pages, dtype=jnp.int32)
    used = place[None, :] * page_len < lengths[:, None]
    match = (page_table[:, :, None] == slots) & used[:, :, None]
    owns = jnp.any(match, axis=1)
    owner = jnp.sum(
        jnp.where(owns, jnp.arange(requests, dtype=jnp.int32)[:, None], 0), axis=0
    )
    left = lengths[:, None] - place[None, :] * page_len
    limit = jnp.sum(jnp.where(match, left[:, :, None], 0), axis=(0, 1))
    asked = queries[owner]

    def page_part(pages, lo, hi):
        scores = (
            jnp.einsum("shc,skc->shk", asked[lo:hi], pages, preferred_element_type=f32)
            * score_scale
        )
        position = jnp.arange(page_len, dtype=jnp.int32)
        scores = jnp.where(position[None, None, :] < limit[lo:hi, None, None], scores, -jnp.inf)
        highest = jnp.max(scores, axis=-1, keepdims=True)
        exponent = jnp.exp(scores - highest)
        total = jnp.sum(exponent, axis=-1)
        part = jnp.einsum(
            "shk,skl->shl", exponent.astype(bf16), pages[:, :, :latent], preferred_element_type=f32
        ).astype(bf16)
        return highest[:, :, 0], total, part

    m0, l0, o0 = page_part(kv_cache[:local_count], 0, local_count)
    m1, l1, o1 = page_part(moved, local_count, pages_dev)
    highest = jnp.concatenate([m0, m1], 0).T
    total = jnp.concatenate([l0, l1], 0).T
    part = jnp.concatenate([o0, o1], 0)
    own = owns[None, :, :]
    peak = jnp.max(jnp.where(own, highest[:, None, :], -jnp.inf), axis=-1, keepdims=True)
    factor = jnp.where(own, jnp.exp(jnp.where(own, highest[:, None, :] - peak, 0.0)), 0.0)
    mass = jnp.sum(factor * total[:, None, :], axis=-1, keepdims=True)
    share = (factor / mass).astype(bf16)
    context = jnp.einsum("hrs,shl->hrl", share, part, preferred_element_type=f32).astype(bf16)
    heads_out = jnp.einsum("hrl,hlv->rhv", context, value_up, preferred_element_type=f32)
    heads_out = heads_out.astype(bf16).reshape(requests, -1)

    width = stream.shape[1] // 2
    stream_half = lax.dynamic_slice_in_dim(stream, t * width, width, 1)
    hidden = project(heads_out, output_weight, stream_half, pairs)

    route = routes[:, 0]
    onehot = (route[:, None] == jnp.arange(pairs, dtype=jnp.int32)[None, :]).astype(jnp.int32)
    rank = jnp.sum((jnp.cumsum(onehot, axis=0) - onehot) * onehot, axis=1)
    seats = jnp.arange(CAP, dtype=jnp.int32)
    named = route[None, :] == jnp.arange(pairs, dtype=jnp.int32)[:, None]
    pick = ((rank[None, None, :] == seats[None, :, None]) & named[:, None, :]).astype(bf16)
    put = ((rank[None, :, None] == seats[None, None, :]) & named[:, :, None]).astype(bf16)
    return run_experts(hidden, pick, put, norm_gain, gate_weight, up_weight, down_weight, pairs)


def solution(mesh):
    in_specs = (
        P(("group", "afd"), None, None),
        P(("group", "afd"), "tensor", None),
        P("group", "afd"),
        P(("group", "afd"), None),
        P(("group", "afd")),
        P(("group", "afd"), None),
        P("group", None),
        P("tensor", None, None),
        P("tensor", "afd"),
        P(),
        P(None, ("afd", "tensor")),
        P(None, ("afd", "tensor")),
        P(("afd", "tensor"), None),
    )
    out_specs = P("group", ("afd", "tensor"))
    return jax.shard_map(
        on_device, mesh=mesh, in_specs=in_specs, out_specs=out_specs, check_vma=False
    )
```

time: 495 us -> 189 us (0.38)
  the two profiles are of different devices: /device:TPU:13 before, /device:TPU:0 now
where the time goes in v1:
time: 189 us; the launch traced here: 188 us
  Pallas kernels  148 us (78%)
  local copies, waits for them, and re-layouts  15.8 us (8%)
  other arithmetic  12.2 us (6%)
  matrix products  12 us (6%)
    pallas_call x1, Pallas kernels, run_experts(): pl.pallas_call(functools.partial(experts_kernel, pairs), out_shape=jax.Sh...  77.5 us
    pallas_call x1, Pallas kernels, project(): pl.pallas_call(functools.partial(project_kernel, pairs), out_shape=jax.Sh...  52.6 us
    pallas_call x1, Pallas kernels, exchange_pages(): pl.pallas_call(functools.partial(pages_kernel, count), out_shape=jax.Shap...  18 us
    dot_general x1, matrix products, on_device(): jnp.einsum('hrl,hlv->rhv', context, value_up, preferred_element_type=f32)  6.26 us

profile of v1, /device:TPU:0, one launch (start us, length us, event | category | flops | bytes accessed | tf_op | source)
XLA Modules:
  0.0 188.3 jit_solution(11793329967761499402)
XLA Ops:
  0.0 0.8 fusion.55
  0.8 3.8 %gather_fusion.1 = bf16[8,64,576]{2,1,0:T(8,128)(2,1)} fusion(bf16[56,64,576]{2,1,0:T(8,128)(2,1)} %param.13, s32[1024]{0:T(1024)S(1)} %pad_clamp_fusion), kind=kCustom, calls=%fused_computation.1 | custom fusion | bytes 1179680 | tf_op jit(solution)/shard_map/gather | solution.py:445
  4.6 1.1 copy-done.1
  5.7 18.0 %shard_map.127 = bf16[8,2,1,64,576]{4,3,2,1,0:T(8,128)(2,1)S(1)} custom-call(bf16[8,1,64,576]{3,2,1,0:T(8,128)(2,1)S(1)} %bitcast.47), custom_call_target="tpu_custom_call" | custom-call | tf_op jit(solution)/shard_map/pallas_call | solution.py:69
  24.1 2.3 %gather_fusion = bf16[56,32,576]{2,1,0:T(8,128)(2,1)} fusion(bf16[48,32,576]{2,1,0:T(8,128)(2,1)S(1)} %copy-done, s32[1024]{0:T(1024)S(1)} %pad_clamp_fusion.1), kind=kCustom, calls=%fused_computation | custom fusion | bytes 4128992 | tf_op jit(solution)/shard_map/gather | solution.py:457
  26.9 1.8 fusion.57
  29.2 0.8 copy-done.3
  30.0 1.2 fusion.58
  31.2 0.8 copy-done.4
  33.1 1.4 copy.30
  34.5 1.3 maximum_bitcast_fusion
  35.9 1.4 copy.29
  37.3 2.6 %multiply_reduce_fusion = (f32[32,48]{1,0:T(8,128)}, f32[32,48,56]{2,1,0:T(8,128)}) fusion(f32[32,56]{1,0:T(8,128)} %copy.30, f32[32,56]{1,0:T(8,128)} %copy.29, pred[48,56]{1,0:T(8,128)(4,1)S(1)} %fusion.47), kind=kOutput, calls=%fused_computation.30 | output fusion | flops 516151 | bytes 367232 | tf_op jit(solution)/shard_map/sub | solution.py:481
  40.3 2.3 %fusion.10 = bf16[40,32,512]{2,1,0:T(8,128)(2,1)S(1)} fusion(bf16[56,64,576]{2,1,0:T(8,128)(2,1)} %param.13, f32[40,32,64]{2,1,0:T(8,128)S(1)} %copy-done.5, f32[40,32]{1,0:T(8,128)S(1)} %copy-done.7), kind=kOutput, calls=%fused_computation.11 | convolution fusion | flops 84705280 | bytes 4264960 | tf_op jit(solution)/shard_map/shk,skl->shl/dot_general | solution.py:469
  42.6 1.4 pad_maximum_fusion
  44.0 6.3 %fusion.29 = bf16[32,6,8,128]{3,2,1,0:T(8,128)(2,1)S(1)} fusion(bf16[32,512,128]{2,1,0:T(8,128)(2,1)} %param.20, bf16[56,32,512]{2,1,0:T(8,128)(2,1)} %pad_maximum_fusion, f32[32,48,56]{2,1,0:T(8,128)} %get-tuple-element.10, f32[32,48]{1,0:T(8,128)S(1)} %copy-done.13), kind=kOutput, calls=%fused_computation.23 | convolution fusion | flops 290562048 | bytes 6772736 | tf_op jit(solution)/shard_map/hrl,hlv->rhv/dot_general | solution.py:485
  50.7 52.6 %shard_map.128.hidden_ref = bf16[384,448]{1,0:T(8,128)(2,1)S(1)} custom-call(bf16[48,4096]{1,0:T(8,128)(2,1)S(1)} %bitcast.48, bf16[4096,896]{1,0:T(8,128)(2,1)} %w_hbm.1, bf16[384,448]{1,0:T(8,128)(2,1)S(1)} %constant_dynamic-slice_fusion.stream_ref), custom_call_target="tpu_custom_call" | custom-call | tf_op jit(solution)/shard_map/pallas_call | solution.py:183
  103.3 0.7 copy-done.2
  104.1 1.2 reduce-window.6
  105.9 1.2 and_convert_fusion.place_ref
  107.2 1.0 and_convert_fusion.1.pick_ref
  108.2 0.7 reshape.242.gain_ref
  108.9 77.5 %shard_map.129 = bf16[384,448]{1,0:T(8,128)(2,1)} custom-call(bf16[384,448]{1,0:T(8,128)(2,1)} %copy-done.2, bf16[4,240,384]{2,1,0:T(8,128)(2,1)} %and_convert_fusion.1.pick_ref, bf16[4,384,240]{2,1,0:T(8,128)(2,1)} %and_convert_fusion.place_ref, f32[16,1,448]{2,1,0:T(1,128)} %reshape.242.gain_ref, bf16[16,448,256]{2,1,0:T(8,128)(2,1)} %bitcast.51, ...), custom_call_target="tpu_custom_call" | custom-call | tf_op jit(solution)/shard_map/pallas_call | solution.py:379
  186.4 1.9 %copy.33 = bf16[384,448]{0,1:T(8,128)(2,1)} copy(bf16[384,448]{1,0:T(8,128)(2,1)} %shard_map.129) | data formatting | bytes 688128 | tf_op jit(solution)/shard_map/pallas_call | solution.py:379
  (57 shorter events, 3.8 us)
Async XLA Ops:
  0.0 24.1 %copy-start = (bf16[48,32,576]{2,1,0:T(8,128)(2,1)S(1)}, bf16[48,32,576]{2,1,0:T(8,128)(2,1)}, u32[]{:S(2)}) copy-start(bf16[48,32,576]{2,1,0:T(8,128)(2,1)} %param.14) | copy-start | bytes 5308420
  0.0 23.7 %copy-start.11 = (s32[48]{0:T(128)S(1)}, s32[48]{0:T(128)}, u32[]{:S(2)}) copy-start(s32[48]{0:T(128)} %param.17) | copy-start | bytes 580
  0.0 23.8 %copy-start.10 = (s32[48,8]{0,1:T(8,128)S(1)}, s32[48,8]{0,1:T(8,128)}, u32[]{:S(2)}) copy-start(s32[48,8]{0,1:T(8,128)} %param.16) | copy-start | bytes 4612
  4.6 1.1 copy-start.1
  26.8 2.4 %slice-start = ((s8[4587520]{0:T(1024)(128)(4,1)}), s8[4194304]{0:T(1024)(128)(4,1)S(1)}, s32[]{:S(2)}) async-start(s8[4587520]{0:T(1024)(128)(4,1)} %bitcast.49), calls=%async_computation | async-start | bytes 8388608
  26.9 3.1 %copy-start.3 = (bf16[56,32,576]{2,1,0:T(8,128)(2,1)S(1)}, bf16[56,32,576]{2,1,0:T(8,128)(2,1)}, u32[]{:S(2)}) copy-start(bf16[56,32,576]{2,1,0:T(8,128)(2,1)} %gather_fusion) | copy-start | bytes 6193156
  26.9 3.1 %slice-start.1 = ((s8[4587520]{0:T(1024)(128)(4,1)}), s8[393216]{0:T(1024)(128)(4,1)S(1)}, s32[]{:S(2)}) async-start(s8[4587520]{0:T(1024)(128)(4,1)} %bitcast.49), calls=%async_computation.1 | async-start | bytes 786432
  31.2 0.8 copy-start.4
  31.2 1.3 copy-start.6
  37.3 3.0 %copy-start.5 = (f32[40,32,64]{2,1,0:T(8,128)S(1)}, f32[40,32,64]{2,1,0:T(8,128)}, u32[]{:S(2)}) copy-start(f32[40,32,64]{2,1,0:T(8,128)} %copy-done.4) | copy-start | bytes 983044
  37.3 3.0 %copy-start.7 = (f32[40,32]{1,0:T(8,128)S(1)}, f32[40,32]{1,0:T(8,128)}, u32[]{:S(2)}) copy-start(f32[40,32]{1,0:T(8,128)} %copy-done.6) | copy-start | bytes 15364
  42.6 1.4 copy-start.13
  44.0 6.4 %copy-start.8 = (bf16[384,896]{1,0:T(8,128)(2,1)S(1)}, bf16[384,896]{1,0:T(8,128)(2,1)}, u32[]{:S(2)}) copy-start(bf16[384,896]{1,0:T(8,128)(2,1)} %param.15) | copy-start | bytes 2064388
  50.6 53.4 %copy-start.12 = (s32[384,1]{0,1:T(1,128)S(1)}, s32[384,1]{0,1:T(1,128)}, u32[]{:S(2)}) copy-start(s32[384,1]{0,1:T(1,128)} %param.19) | copy-start | bytes 4612
  50.6 57.6 %copy-start.9 = (f32[7168]{0:T(1024)S(1)}, f32[7168]{0:T(1024)}, u32[]{:S(2)}) copy-start(f32[7168]{0:T(1024)} %param.22) | copy-start | bytes 86020
  103.3 0.7 copy-start.2

commit v2 on v1

--- a/solution.py
+++ b/solution.py
@@ -39,43 +39,110 @@
     pl.semaphore_wait(barrier, len(targets))
 
 
-def pages_kernel(count, out_ref, got_ref, sent_sem, got_sem, pass_sem, passed_sem, own_sem):
+def attend_kernel(
+    count, each, local, owner_ref, limit_ref, give_ref, kv_ref, q_ref, part_ref, top_ref, mass_ref,
+    out, got, sent_sem, got_sem, pass_sem, passed_sem,
+):
     me = lax.axis_index("afd")
     t = lax.axis_index("tensor")
     greet([(lax.rem(me + d, count), t) for d in range(1, count)] + [(me, 1 - t)])
+    latent = part_ref.shape[2]
+
+    def page_to(to):
+        return send(out.at[to], got.at[me, t], sent_sem.at[to], got_sem.at[me], to, t)
+
+    def page_from(src):
+        return send(out.at[src], got.at[src, t], sent_sem.at[src], got_sem.at[src], src, t)
+
+    def swap(src, side):
+        return send(got.at[src, side], got.at[src, side], pass_sem.at[src], passed_sem.at[src], me, 1 - t)
+
     for d in range(1, count):
         to = lax.rem(me + d, count)
-        send(out_ref.at[to], got_ref.at[me, t], sent_sem.at[to], got_sem.at[me], to, t).start()
-    own = pltpu.make_async_copy(out_ref.at[me], got_ref.at[me, t], own_sem)
-    own.start()
-    own.wait()
+        for j in range(each):
+            out[to, j] = kv_ref[give_ref[to * each + j]]
+        page_to(to).start()
+    for j in range(each):
+        got[me, t, j] = kv_ref[give_ref[me * each + j]]
+    swap(me, t).start()
+
+    def one(slot, page):
+        scores = lax.dot_general(
+            page, q_ref[owner_ref[slot]], (((1,), (1,)), ((), ())), preferred_element_type=f32
+        ) * score_scale
+        position = lax.broadcasted_iota(jnp.int32, scores.shape, 0)
+        scores = jnp.where(position < limit_ref[slot], scores, -jnp.inf)
+        top = jnp.max(scores, axis=0, keepdims=True)
+        exponent = jnp.exp(scores - top)
+        top_ref[slot] = top
+        mass_ref[slot] = jnp.sum(exponent, axis=0, keepdims=True)
+        part_ref[slot] = lax.dot_general(
+            exponent.astype(bf16), page[:, :latent], (((0,), (0,)), ((), ())),
+            preferred_element_type=f32,
+        ).astype(bf16)
+
+    def forward(d):
+        src = lax.rem(me + d, count)
+        page_from(src).wait_recv()
+        swap(src, t).start()
+
+    pace = local // count
+
+    def resident(i, carry):
+        for j in range(pace):
+            one(i * pace + j, kv_ref[i * pace + j])
+        return carry
+
+    def resident_and_forward(i, carry):
+        resident(i, carry)
+        forward(i)
+        return carry
+
+    resident(0, 0)
+    lax.fori_loop(1, count, resident_and_forward, 0)
+    for slot in range(pace * count, local):
+        one(slot, kv_ref[slot])
+
+    def arrived(d, carry):
+        src = lax.rem(me + d, count)
+        swap(src, 1 - t).wait_recv()
+        for side in range(2):
+            for j in range(each):
+                one(local + (src * 2 + side) * each + j, got[src, side, j])
+        return carry
+
+    lax.fori_loop(0, count, arrived, 0)
     for d in range(count):
-        src = lax.rem(me + count - d, count)
+        to = lax.rem(me + d, count)
+        swap(to, t).wait_send()
         if d > 0:
-            send(out_ref.at[src], got_ref.at[src, t], sent_sem.at[src], got_sem.at[src], src, t).wait_recv()
-        send(got_ref.at[src, t], got_ref.at[src, t], pass_sem.at[src], passed_sem.at[src], me, 1 - t).start()
-    for d in range(count):
-        src = lax.rem(me + count - d, count)
-        back = send(got_ref.at[src, 1 - t], got_ref.at[src, 1 - t], pass_sem.at[src], passed_sem.at[src], me, 1 - t)
-        back.wait_recv()
-        back.wait_send()
-    for d in range(1, count):
-        to = lax.rem(me + d, count)
-        send(out_ref.at[to], got_ref.at[me, t], sent_sem.at[to], got_sem.at[me], to, t).wait_send()
-
-
-def exchange_pages(outgoing, count):
+            page_to(to).wait_send()
+
+
+def attend(kv_cache, queries, owner, limit, give, count, each, local, latent):
     dma = pltpu.SemaphoreType.DMA
+    slots, page_len, channels = kv_cache.shape
+    heads = queries.shape[1]
+    vmem = pl.BlockSpec(memory_space=pltpu.VMEM)
+    smem = pl.BlockSpec(memory_space=pltpu.SMEM)
     return pl.pallas_call(
-        functools.partial(pages_kernel, count),
-        out_shape=jax.ShapeDtypeStruct((count, 2) + outgoing.shape[1:], bf16),
-        in_specs=[pl.BlockSpec(memory_space=pltpu.VMEM)],
-        out_specs=pl.BlockSpec(memory_space=pltpu.VMEM),
-        scratch_shapes=[dma((count,)), dma((count,)), dma((count,)), dma((count,)), dma],
+        functools.partial(attend_kernel, count, each, local),
+        out_shape=(
+            jax.ShapeDtypeStruct((slots, heads, latent), bf16),
+            jax.ShapeDtypeStruct((slots, 1, heads), f32),
+            jax.ShapeDtypeStruct((slots, 1, heads), f32),
+        ),
+        in_specs=[smem, smem, smem, vmem, vmem],
+        out_specs=(vmem, vmem, vmem),
+        scratch_shapes=[
+            pltpu.VMEM((count, each, page_len, channels), bf16),
+            pltpu.VMEM((count, 2, each, page_len, channels), bf16),
+            dma((count,)), dma((count,)), dma((count,)), dma((count,)),
+        ],
         compiler_params=pltpu.CompilerParams(
             collective_id=0, has_side_effects=True, vmem_limit_bytes=40 * 2**20
         ),
-    )(outgoing)
+    )(owner, limit, give, kv_cache, queries)
 
 
 def project_kernel(
@@ -91,78 +158,86 @@
         [(2 * lax.rem(z + d, pairs) + y, t) for d in range(1, pairs)]
         + [(2 * z + 1 - y, t), (me, 1 - t)]
     )
-    held[me] = heads_ref[...]
-
-    def side(slot):
-        return send(held.at[slot], held.at[slot], side_sem.at[slot // 2], got_sem.at[slot], 2 * z + 1 - y, t)
-
-    def up(slot):
-        return send(held.at[slot], held.at[slot], up_sem.at[slot // 2], got_sem.at[slot], me + 2, t)
-
-    def down(slot):
-        return send(held.at[slot], held.at[slot], down_sem.at[slot // 2], got_sem.at[slot], me - 2, t)
-
-    @pl.when(z + 1 < pairs)
-    def _():
-        up(me).start()
-
-    @pl.when(z > 0)
-    def _():
-        down(me).start()
-
-    side(me).start()
-    for s in range(1, pairs):
-
+    chunks, count, rows, step = held.shape
+
+    def side(c, slot):
+        here = held.at[c, slot]
+        return send(here, here, side_sem.at[c, slot // 2], got_sem.at[c, slot], 2 * z + 1 - y, t)
+
+    def up(c, slot):
+        here = held.at[c, slot]
+        return send(here, here, up_sem.at[c, slot // 2], got_sem.at[c, slot], me + 2, t)
+
+    def down(c, slot):
+        here = held.at[c, slot]
+        return send(here, here, down_sem.at[c, slot // 2], got_sem.at[c, slot], me - 2, t)
+
+    def begin(c):
+        held[c, me] = heads_ref[:, c * step : (c + 1) * step]
+
+        @pl.when(z + 1 < pairs)
+        def _():
+            up(c, me).start()
+
+        @pl.when(z > 0)
+        def _():
+            down(c, me).start()
+
+        side(c, me).start()
+
+    def relay(c, s):
         @pl.when(z - s >= 0)
         def _():
             slot = me - 2 * s
-            up(slot).wait_recv()
+            up(c, slot).wait_recv()
 
             @pl.when(z + 1 < pairs)
             def _():
-                up(slot).start()
-
-            side(slot).start()
+                up(c, slot).start()
+
+            side(c, slot).start()
 
         @pl.when(z + s < pairs)
         def _():
             slot = me + 2 * s
-            down(slot).wait_recv()
+            down(c, slot).wait_recv()
 
             @pl.when(z > 0)
             def _():
-                down(slot).start()
-
-            side(slot).start()
-
-    for a in range(pairs):
-        slot = 2 * a + 1 - y
-        side(slot).wait_recv()
-    for a in range(pairs):
-        slot = 2 * a + y
-        side(slot).wait_send()
-
-        @pl.when((a <= z) & (z + 1 < pairs))
-        def _():
-            up(slot).wait_send()
-
-        @pl.when((a >= z) & (z > 0))
-        def _():
-            down(slot).wait_send()
-
-    load.wait()
-    count, rows, depth = held.shape
-    step = 512
+                down(c, slot).start()
+
+            side(c, slot).start()
+
+    def finish(c):
+        for a in range(pairs):
+            side(c, 2 * a + 1 - y).wait_recv()
+        block = held[c].reshape(count * rows, step)
+        acc[...] += jnp.dot(block, w[c * step : (c + 1) * step, :], preferred_element_type=f32)
+
     acc[...] = jnp.zeros_like(acc)
-
-    def body(k, carry):
-        at = pl.ds(pl.multiple_of(k * step, step), step)
-        acc[...] += jnp.dot(
-            held[:, :, at].reshape(count * rows, step), w[at, :], preferred_element_type=f32
-        )
-        return carry
-
-    lax.fori_loop(0, depth // step, body, 0)
+    for turn in range(chunks + pairs):
+        if turn < chunks:
+            begin(turn)
+        for s in range(pairs - 1, 0, -1):
+            if 0 <= turn - s < chunks:
+                relay(turn - s, s)
+        if turn == pairs:
+            load.wait()
+        if turn >= pairs:
+            finish(turn - pairs)
+    for c in range(chunks):
+        for a in range(pairs):
+            slot = 2 * a + y
+            side(c, slot).wait_send()
+
+            @pl.when((a <= z) & (z + 1 < pairs))
+            def _():
+                up(c, slot).wait_send()
+
+            @pl.when((a >= z) & (z > 0))
+            def _():
+                down(c, slot).wait_send()
+
     width = half_out.shape[1]
     total = acc[...]
     left, right = total[:, :width], total[:, width:]
@@ -179,6 +254,7 @@
     dma = pltpu.SemaphoreType.DMA
     rows, depth = heads.shape
     tokens, width = stream_half.shape
+    chunks = 4
     vmem = pl.BlockSpec(memory_space=pltpu.VMEM)
     return pl.pallas_call(
         functools.partial(project_kernel, pairs),
@@ -186,16 +262,16 @@
         in_specs=[vmem, pl.BlockSpec(memory_space=pl.ANY), vmem],
         out_specs=vmem,
         scratch_shapes=[
-            pltpu.VMEM((2 * pairs, rows, depth), bf16),
+            pltpu.VMEM((chunks, 2 * pairs, rows, depth // chunks), bf16),
             pltpu.VMEM(weight.shape, bf16),
             pltpu.VMEM((tokens, 2 * width), f32),
             pltpu.VMEM((tokens, width), f32),
             pltpu.VMEM((tokens, width), f32),
             dma,
-            dma((2 * pairs,)),
-            dma((pairs,)),
-            dma((pairs,)),
-            dma((pairs,)),
+            dma((chunks, 2 * pairs)),
+            dma((chunks, pairs)),
+            dma((chunks, pairs)),
+            dma((chunks, pairs)),
             dma((2,)),
         ],
         compiler_params=pltpu.CompilerParams(
@@ -441,8 +517,7 @@
     latent = value_up.shape[1]
     each = migrate_count // 2
 
-    mine = lax.dynamic_slice_in_dim(send_pages, t * each, each, 1)
-    moved = exchange_pages(kv_cache[mine], afd_count).reshape(moved_total, page_len, channels)
+    give = lax.dynamic_slice_in_dim(send_pages, t * each, each, 1).reshape(-1)
 
     slots = jnp.arange(pages_dev, dtype=jnp.int32)
     place = jnp.arange(max_pages, dtype=jnp.int32)
@@ -454,28 +529,11 @@
     )
     left = lengths[:, None] - place[None, :] * page_len
     limit = jnp.sum(jnp.where(match, left[:, :, None], 0), axis=(0, 1))
-    asked = queries[owner]
-
-    def page_part(pages, lo, hi):
-        scores = (
-            jnp.einsum("shc,skc->shk", asked[lo:hi], pages, preferred_element_type=f32)
-            * score_scale
-        )
-        position = jnp.arange(page_len, dtype=jnp.int32)
-        scores = jnp.where(position[None, None, :] < limit[lo:hi, None, None], scores, -jnp.inf)
-        highest = jnp.max(scores, axis=-1, keepdims=True)
-        exponent = jnp.exp(scores - highest)
-        total = jnp.sum(exponent, axis=-1)
-        part = jnp.einsum(
-            "shk,skl->shl", exponent.astype(bf16), pages[:, :, :latent], preferred_element_type=f32
-        ).astype(bf16)
-        return highest[:, :, 0], total, part
-
-    m0, l0, o0 = page_part(kv_cache[:local_count], 0, local_count)
-    m1, l1, o1 = page_part(moved, local_count, pages_dev)
-    highest = jnp.concatenate([m0, m1], 0).T
-    total = jnp.concatenate([l0, l1], 0).T
-    part = jnp.concatenate([o0, o1], 0)
+    part, highest, total = attend(
+        kv_cache, queries, owner, limit, give, afd_count, each, local_count, latent
+    )
+    highest = highest[:, 0].T
+    total = total[:, 0].T
     own = owns[None, :, :]
     peak = jnp.max(jnp.where(own, highest[:, None, :], -jnp.inf), axis=-1, keepdims=True)
     factor = jnp.where(own, jnp.exp(jnp.where(own, highest[:, None, :] - peak, 0.0)), 0.0)

time: 189 us -> 176 us (0.931)
  local copies, waits for them, and re-layouts: 15.8 us -> 9.39 us
  matrix products: 12 us -> 5.66 us
  other arithmetic: 12.2 us -> 7.02 us
  Pallas kernels: 148 us -> 153 us
    pallas_call x1, Pallas kernels: 18 us -> 25.8 us  [attend(): pl.pallas_call(functools.partial(attend_kernel, count, each, local), out_...]
    gather x2 -> x0, local copies, waits for them, and re-layouts: 6.06 us -> none  [the longest x1 3.76 us: on_device(): kv_cache[mine]]
    dot_general x4 -> x0, matrix products: 5.71 us -> none  [the longest x2 3.05 us: page_part(): jnp.einsum('shc,skc->shk', asked[lo:hi], pages, preferred_element_type=f32)]
    pallas_call x1, Pallas kernels: 52.6 us -> 49.9 us  [project(): pl.pallas_call(functools.partial(project_kernel, pairs), out_shape=jax.Sh...]
    transpose x2, local copies, waits for them, and re-layouts: 2.84 us -> 0.14 us  [the longest x1 0.07 us: on_device(): total = total[:, 0].T]
    transpose x2 -> x0, other arithmetic: 1.96 us -> none  [the longest x1 1.34 us: on_device(): highest = jnp.concatenate([m0, m1], 0).T]
    unnamed x33 -> x13, local copies, waits for them, and re-layouts: 3.66 us -> 5.36 us
where the time goes in v2:
time: 176 us
  Pallas kernels  153 us (87%)
  local copies, waits for them, and re-layouts  9.39 us (5%)
  other arithmetic  7.02 us (4%)
  matrix products  5.66 us (3%)
    pallas_call x1, Pallas kernels, run_experts(): pl.pallas_call(functools.partial(experts_kernel, pairs), out_shape=jax.Sh...  77.8 us
    pallas_call x1, Pallas kernels, project(): pl.pallas_call(functools.partial(project_kernel, pairs), out_shape=jax.Sh...  49.9 us
    pallas_call x1, Pallas kernels, attend(): pl.pallas_call(functools.partial(attend_kernel, count, each, local), out_...  25.8 us
    dot_general x1, matrix products, on_device(): jnp.einsum('hrl,hlv->rhv', context, value_up, preferred_element_type=f32)  5.66 us
    unnamed x13, local copies, waits for them, and re-layouts  5.36 us

profile of v2, /device:TPU:0, one launch (start us, length us, event | category | flops | bytes accessed | tf_op | source)
XLA Modules:
  0.0 175.7 jit_solution(11128508787551451684)
XLA Ops:
  0.0 0.8 dynamic-slice_bitcast_fusion.give_ref
  0.8 0.7 broadcast_compare_fusion
  1.5 0.7 broadcast_subtract_fusion
  2.2 0.8 copy.24
  3.0 0.2 select_reduce_fusion.1.limit_ref
  3.2 0.2 fusion.26
  3.4 2.3 %copy-done.1 = bf16[56,64,576]{2,1,0:T(8,128)(2,1)S(1)} copy-done((bf16[56,64,576]{2,1,0:T(8,128)(2,1)S(1)}, bf16[56,64,576]{2,1,0:T(8,128)(2,1)}, u32[]{:S(2)}) %copy-start.1) | copy-done | bytes 4128792
  5.7 1.5 copy-done.2
  7.3 25.8 %shard_map.127 = (bf16[56,32,512]{2,1,0:T(8,128)(2,1)S(1)}, f32[56,1,32]{2,1,0:T(1,128)S(1)}, f32[56,1,32]{2,1,0:T(1,128)S(1)}) custom-call(s32[56]{0:T(128)S(1)} %select_reduce_fusion.2.owner_ref, s32[56]{0:T(128)S(1)} %select_reduce_fusion.1.limit_ref, s32[8]{0:T(128)S(1)} %dynamic-slice_bitcast_fusion.give_ref, bf16[56,64,576]{2,1,0:T(8,128)(2,1)S(1)} %copy-done.1, ...), custom_call_target="tpu_custom_call" | custom-call | tf_op jit(solution)/shard_map/pallas_call | solution.py:128
  33.2 1.2 multiply_reduce_fusion
  34.4 5.7 %fusion.16 = bf16[32,6,8,128]{3,2,1,0:T(8,128)(2,1)S(1)} fusion(bf16[32,512,128]{2,1,0:T(8,128)(2,1)} %param.20, bf16[56,32,512]{2,1,0:T(8,128)(2,1)S(1)} %get-tuple-element.10, f32[32,48,56]{2,1,0:T(8,128)} %get-tuple-element.12, f32[32,48]{1,0:T(8,128)S(1)} %get-tuple-element.11), kind=kOutput, calls=%fused_computation.12 | convolution fusion | flops 290562048 | bytes 6772736 | tf_op jit(solution)/shard_map/hrl,hlv->rhv/dot_general | solution.py:543
  40.2 0.2 constant_dynamic-slice_fusion.stream_ref
  40.4 49.9 %shard_map.128.hidden_ref = bf16[384,448]{1,0:T(8,128)(2,1)S(1)} custom-call(bf16[48,4096]{1,0:T(8,128)(2,1)S(1)} %bitcast.37, bf16[4096,896]{1,0:T(8,128)(2,1)} %w_hbm.1, bf16[384,448]{1,0:T(8,128)(2,1)S(1)} %constant_dynamic-slice_fusion.stream_ref), custom_call_target="tpu_custom_call" | custom-call | tf_op jit(solution)/shard_map/pallas_call | solution.py:259
  90.4 0.7 copy-done.3
  91.2 1.2 reduce-window.6
  92.4 0.2 slice_reduce_fusion
  92.6 0.2 reduce-window.9
  92.8 0.1 add_bitcast_fusion
  92.9 0.1 iota_compare_fusion
  93.0 1.2 and_convert_fusion.place_ref
  94.2 1.0 and_convert_fusion.1.pick_ref
  95.3 0.7 reshape.185.gain_ref
  96.0 77.8 %shard_map.129 = bf16[384,448]{1,0:T(8,128)(2,1)} custom-call(bf16[384,448]{1,0:T(8,128)(2,1)} %copy-done.3, bf16[4,240,384]{2,1,0:T(8,128)(2,1)} %and_convert_fusion.1.pick_ref, bf16[4,384,240]{2,1,0:T(8,128)(2,1)} %and_convert_fusion.place_ref, f32[16,1,448]{2,1,0:T(1,128)} %reshape.185.gain_ref, bf16[16,448,256]{2,1,0:T(8,128)(2,1)} %bitcast.40, ...), custom_call_target="tpu_custom_call" | custom-call | tf_op jit(solution)/shard_map/pallas_call | solution.py:455
  173.8 1.9 %copy.29 = bf16[384,448]{0,1:T(8,128)(2,1)} copy(bf16[384,448]{1,0:T(8,128)(2,1)} %shard_map.129) | data formatting | bytes 688128 | tf_op jit(solution)/shard_map/pallas_call | solution.py:455
  (19 shorter events, 0.4 us)
Async XLA Ops:
  0.0 40.2 %copy-start = (bf16[384,896]{1,0:T(8,128)(2,1)S(1)}, bf16[384,896]{1,0:T(8,128)(2,1)}, u32[]{:S(2)}) copy-start(bf16[384,896]{1,0:T(8,128)(2,1)} %param.15) | copy-start | bytes 2064388
  3.4 2.3 %copy-start.1 = (bf16[56,64,576]{2,1,0:T(8,128)(2,1)S(1)}, bf16[56,64,576]{2,1,0:T(8,128)(2,1)}, u32[]{:S(2)}) copy-start(bf16[56,64,576]{2,1,0:T(8,128)(2,1)} %kv_ref.1) | copy-start | bytes 12386308
  5.7 1.5 copy-start.2
  40.4 50.7 %copy-start.5 = (s32[384,1]{0,1:T(1,128)S(1)}, s32[384,1]{0,1:T(1,128)}, u32[]{:S(2)}) copy-start(s32[384,1]{0,1:T(1,128)} %param.19) | copy-start | bytes 4612
  40.4 54.9 %copy-start.4 = (f32[7168]{0:T(1024)S(1)}, f32[7168]{0:T(1024)}, u32[]{:S(2)}) copy-start(f32[7168]{0:T(1024)} %param.22) | copy-start | bytes 86020
  90.4 0.7 copy-start.3

commit v3 on v2

--- a/solution.py
+++ b/solution.py
@@ -147,7 +147,7 @@
 
 def project_kernel(
     pairs, heads_ref, w_hbm, stream_ref, hidden_ref,
-    held, w, acc, half_out, half_in, w_sem, got_sem, up_sem, down_sem, side_sem, half_sems,
+    held, w, acc, half_out, half_in, w_sem, got_sem, up_sem, down_sem, side_sem, cross_sem, half_sems,
 ):
     me = lax.axis_index("afd")
     t = lax.axis_index("tensor")
@@ -185,7 +185,30 @@
 
         side(c, me).start()
 
+    mate = z + 1 - 2 * lax.rem(z, 2)
+
+    def cross(c):
+        here = held.at[c, 2 * z + 1 - y]
+        return send(here, here, cross_sem.at[c], got_sem.at[c, 2 * z + 1 - y], 2 * mate + y, t)
+
+    def crosses(c):
+        return c % 2 == 1
+
+    def beside(c, slot):
+        if crosses(c):
+
+            @pl.when(slot // 2 != mate)
+            def _():
+                side(c, slot).start()
+
+        else:
+            side(c, slot).start()
+
     def relay(c, s):
+        if s == 1 and crosses(c):
+            side(c, 2 * z + 1 - y).wait_recv()
+            cross(c).start()
+
         @pl.when(z - s >= 0)
         def _():
             slot = me - 2 * s
@@ -195,7 +218,7 @@
             def _():
                 up(c, slot).start()
 
-            side(c, slot).start()
+            beside(c, slot)
 
         @pl.when(z + s < pairs)
         def _():
@@ -206,11 +229,18 @@
             def _():
                 down(c, slot).start()
 
-            side(c, slot).start()
+            beside(c, slot)
 
     def finish(c):
         for a in range(pairs):
-            side(c, 2 * a + 1 - y).wait_recv()
+            if crosses(c):
+
+                @pl.when(a != z)
+                def _():
+                    side(c, 2 * a + 1 - y).wait_recv()
+
+            else:
+                side(c, 2 * a + 1 - y).wait_recv()
         block = held[c].reshape(count * rows, step)
         acc[...] += jnp.dot(block, w[c * step : (c + 1) * step, :], preferred_element_type=f32)
 
@@ -226,9 +256,18 @@
         if turn >= pairs:
             finish(turn - pairs)
     for c in range(chunks):
+        if crosses(c):
+            cross(c).wait_send()
         for a in range(pairs):
             slot = 2 * a + y
-            side(c, slot).wait_send()
+            if crosses(c):
+
+                @pl.when(a != mate)
+                def _():
+                    side(c, slot).wait_send()
+
+            else:
+                side(c, slot).wait_send()
 
             @pl.when((a <= z) & (z + 1 < pairs))
             def _():
@@ -272,6 +311,7 @@
             dma((chunks, pairs)),
             dma((chunks, pairs)),
             dma((chunks, pairs)),
+            dma((chunks,)),
             dma((2,)),
         ],
         compiler_params=pltpu.CompilerParams(
@@ -281,7 +321,7 @@
 
 
 def experts_kernel(
-    pairs, hidden_ref, pick_ref, place_ref, gain_ref, gate_hbm, up_hbm, down_hbm, out_ref,
+    pairs, hidden_ref, target_row_ref, target_col_ref, gain_ref, gate_hbm, up_hbm, down_hbm, out_ref,
     buf, rows, wg, wu, wd, acc_g, acc_u, squares, term1, send1, got1, send2, got2, send3, got3,
     w_sems, z_sem, row_sem, y_sem, t_sem, sems1, sems2, sems3,
 ):
@@ -301,69 +341,98 @@
         + [(beside, t), (me, 1 - t)]
     )
 
-    def along(e):
-        return send(buf.at[e], rows.at[me, t], z_sem.at[e], row_sem.at[me, t], 2 * e + y, t)
-
-    def across(slot):
-        return send(rows.at[slot, t], rows.at[slot, t], y_sem.at[slot // 2], row_sem.at[slot, t], beside, t)
-
-    def within(slot, side):
-        return send(rows.at[slot, side], rows.at[slot, side], t_sem.at[slot], row_sem.at[slot, side], me, 1 - t)
+    halves = ((0, 128), (128, CAP - 128))
+
+    def along(h, e):
+        at = pl.ds(*halves[h])
+        return send(buf.at[e, at], rows.at[me, t, at], z_sem.at[h, e], row_sem.at[h, me, t], 2 * e + y, t)
+
+    def across(h, slot):
+        here = rows.at[slot, t, pl.ds(*halves[h])]
+        return send(here, here, y_sem.at[h, slot // 2], row_sem.at[h, slot, t], beside, t)
+
+    def within(h, slot, side):
+        here = rows.at[slot, side, pl.ds(*halves[h])]
+        return send(here, here, t_sem.at[h, slot], row_sem.at[h, slot, side], me, 1 - t)
 
     def build(d, carry):
         e = lax.rem(z + d, pairs)
-        buf[e] = jnp.dot(pick_ref[e], hidden_ref[...], preferred_element_type=f32).astype(bf16)
+        seats = lax.broadcasted_iota(jnp.int32, (CAP, target_row_ref.shape[1]), 0) + e * CAP
+        pick = jnp.where(seats == target_row_ref[...], 1.0, 0.0).astype(bf16)
+        buf[e] = jnp.dot(pick, hidden_ref[...], preferred_element_type=f32).astype(bf16)
 
         @pl.when(d < pairs)
         def _():
-            along(e).start()
+            along(0, e).start()
 
         return carry
 
     lax.fori_loop(1, pairs + 1, build, 0)
     rows[me, t] = buf[z]
+    for h in range(2):
+        across(h, me).start()
+        within(h, me, t).start()
     acc_g[...] = jnp.zeros_like(acc_g)
     acc_u[...] = jnp.zeros_like(acc_u)
     squares[...] = jnp.zeros_like(squares)
     loads[0].wait()
     loads[1].wait()
 
-    def work(slot, side):
+    def work(h, slot, side):
         block = slot * 2 + side
-        wide = rows[slot, side].astype(f32)
-        squares[...] += jnp.sum(wide * wide, axis=-1, keepdims=True)
+        lo, size = halves[h]
+        at = slice(lo, lo + size)
+        wide = rows[slot, side, at].astype(f32)
+        squares[at] += jnp.sum(wide * wide, axis=-1, keepdims=True)
         scaled = (wide * gain_ref[block]).astype(bf16)
-        acc_g[...] += jnp.dot(scaled, wg[block], preferred_element_type=f32)
-        acc_u[...] += jnp.dot(scaled, wu[block], preferred_element_type=f32)
-
-    def straight(d, carry):
+        acc_g[at] += jnp.dot(scaled, wg[block], preferred_element_type=f32)
+        acc_u[at] += jnp.dot(scaled, wu[block], preferred_element_type=f32)
+
+    def first_half(d, carry):
+        e = lax.rem(z + d, pairs)
+        slot = 2 * e + y
+        within(0, slot, t).wait_recv()
+        along(1, e).start()
+        across(0, slot).start()
+        within(0, slot, t).start()
+        work(0, slot, t)
+        return carry
+
+    lax.fori_loop(1, pairs, first_half, 0)
+    work(0, me, t)
+    work(1, me, t)
+
+    def second_half(d, carry):
         slot = 2 * lax.rem(z + d, pairs) + y
-
-        @pl.when(d > 0)
-        def _():
-            within(slot, t).wait_recv()
-
-        across(slot).start()
-        within(slot, t).start()
-        work(slot, t)
-        return carry
-
-    lax.fori_loop(0, pairs, straight, 0)
-
-    def sideways(d, carry):
+        within(1, slot, t).wait_recv()
+        across(1, slot).start()
+        within(1, slot, t).start()
+        work(1, slot, t)
+        return carry
+
+    lax.fori_loop(1, pairs, second_half, 0)
+
+    def sideways(h):
+        def body(d, carry):
+            near = 2 * lax.rem(z + d, pairs) + y
+            far = 2 * lax.rem(z + d, pairs) + 1 - y
+            within(h, far, t).wait_recv()
+            within(h, far, t).start()
+            work(h, far, t)
+            within(h, near, 1 - t).wait_recv()
+            work(h, near, 1 - t)
+            return carry
+
+        lax.fori_loop(0, pairs, body, 0)
+
+    sideways(0)
+    sideways(1)
+
+    def swapped(d, carry):
         slot = 2 * lax.rem(z + d, pairs) + 1 - y
-        within(slot, t).wait_recv()
-        within(slot, t).start()
-        work(slot, t)
-        return carry
-
-    lax.fori_loop(0, pairs, sideways, 0)
-
-    def swapped(d, carry):
-        for near in (True, False):
-            slot = 2 * lax.rem(z + d, pairs) + (y if near else 1 - y)
-            within(slot, 1 - t).wait_recv()
-            work(slot, 1 - t)
+        for h in range(2):
+            within(h, slot, 1 - t).wait_recv()
+            work(h, slot, 1 - t)
         return carry
 
     lax.fori_loop(0, pairs, swapped, 0)
@@ -389,15 +458,15 @@
     def swap2(e):
         return send(send2.at[e], got2.at[e], sems2.at[0, e], sems2.at[1, e], beside, t)
 
-    def reduce2(d, carry):
+    def reduce2(d):
         e = lax.rem(z + d, pairs)
         a = 2 * e + 1 - y
         swap1(a).wait_recv()
         send2[e] = (term1[a] + got1[a].astype(f32)).astype(bf16)
         swap2(e).start()
-        return carry
-
-    lax.fori_loop(1, pairs + 1, reduce2, 0)
+
+    reduce2(1)
+    reduce2(2)
 
     def give3(e):
         return send(send3.at[e], got3.at[z], sems3.at[0, e], sems3.at[1, z], 2 * e + y, t)
@@ -410,6 +479,11 @@
         a = 2 * e + y
         swap1(a).wait_recv()
         swap2(e).wait_recv()
+
+        @pl.when(d + 2 <= pairs)
+        def _():
+            reduce2(d + 2)
+
         total = (term1[a] + got1[a].astype(f32) + got2[e].astype(f32)).astype(bf16)
         send3[e] = total
 
@@ -426,21 +500,26 @@
         e = lax.rem(z + d, pairs)
         if d > 0:
             take3(e).wait_recv()
-        mixed += jnp.dot(place_ref[e], got3[e], preferred_element_type=f32)
+        seats = lax.broadcasted_iota(jnp.int32, (mixed.shape[0], CAP), 1) + e * CAP
+        place = jnp.where(seats == target_col_ref[...], 1.0, 0.0).astype(bf16)
+        mixed += jnp.dot(place, got3[e], preferred_element_type=f32)
     out_ref[...] = mixed.astype(bf16)
     for d in range(1, pairs):
         e = lax.rem(z + d, pairs)
-        along(e).wait_send()
         give3(e).wait_send()
+        for h in range(2):
+            along(h, e).wait_send()
     for e in range(pairs):
-        across(2 * e + y).wait_send()
         swap2(e).wait_send()
+        for h in range(2):
+            across(h, 2 * e + y).wait_send()
     for a in range(2 * pairs):
-        within(a, t).wait_send()
         swap1(a).wait_send()
-
-
-def run_experts(hidden, pick, place, gain, gate, up, down, pairs):
+        for h in range(2):
+            within(h, a, t).wait_send()
+
+
+def run_experts(hidden, target, gain, gate, up, down, pairs):
     dma = pltpu.SemaphoreType.DMA
     tokens, width = hidden.shape
     vmem = pl.BlockSpec(memory_space=pltpu.VMEM)
@@ -474,10 +553,10 @@
             tile(pairs),
             tile(pairs),
             dma((3,)),
-            dma((pairs,)),
-            dma((count, 2)),
-            dma((pairs,)),
-            dma((count,)),
+            dma((2, pairs)),
+            dma((2, count, 2)),
+            dma((2, pairs)),
+            dma((2, count)),
             dma((2, count)),
             dma((2, pairs)),
             dma((2, pairs)),
@@ -486,7 +565,7 @@
             collective_id=2, has_side_effects=True, vmem_limit_bytes=56 * 2**20
         ),
     )(
-        hidden, pick, place, gain.reshape(2 * count, 1, width),
+        hidden, target[None, :], target[:, None], gain.reshape(2 * count, 1, width),
         gate.reshape(blocks), up.reshape(blocks), down,
     )
 
@@ -550,11 +629,8 @@
     route = routes[:, 0]
     onehot = (route[:, None] == jnp.arange(pairs, dtype=jnp.int32)[None, :]).astype(jnp.int32)
     rank = jnp.sum((jnp.cumsum(onehot, axis=0) - onehot) * onehot, axis=1)
-    seats = jnp.arange(CAP, dtype=jnp.int32)
-    named = route[None, :] == jnp.arange(pairs, dtype=jnp.int32)[:, None]
-    pick = ((rank[None, None, :] == seats[None, :, None]) & named[:, None, :]).astype(bf16)
-    put = ((rank[None, :, None] == seats[None, None, :]) & named[:, :, None]).astype(bf16)
-    return run_experts(hidden, pick, put, norm_gain, gate_weight, up_weight, down_weight, pairs)
+    target = route * CAP + rank
+    return run_experts(hidden, target, norm_gain, gate_weight, up_weight, down_weight, pairs)
 
 
 def solution(mesh):

time: 176 us -> 171 us (0.972); the launches traced: 176 us -> 168 us
  Pallas kernels: 153 us -> 147 us
    pallas_call x1, Pallas kernels: 77.8 us -> 72.2 us  [run_experts(): pl.pallas_call(functools.partial(experts_kernel, pairs), out_shape=jax.Sh...]
    convert_element_type x2 -> x0, other arithmetic: 2.19 us -> none  [the longest x1 1.15 us: on_device(): ((rank[None, :, None] == seats[None, None, :]) & named[:, :, None]).astyp...]
    unnamed x13 -> x14, local copies, waits for them, and re-layouts: 5.36 us -> 5.5 us
where the time goes in v3:
time: 171 us; the launch traced here: 168 us
  Pallas kernels  147 us (86%)
  local copies, waits for them, and re-layouts  9.51 us (6%)
  other arithmetic  6 us (4%)
  matrix products  5.66 us (3%)
    pallas_call x1, Pallas kernels, run_experts(): pl.pallas_call(functools.partial(experts_kernel, pairs), out_shape=jax.Sh...  72.2 us
    pallas_call x1, Pallas kernels, project(): pl.pallas_call(functools.partial(project_kernel, pairs), out_shape=jax.Sh...  49.1 us
    pallas_call x1, Pallas kernels, attend(): pl.pallas_call(functools.partial(attend_kernel, count, each, local), out_...  25.8 us
    dot_general x1, matrix products, on_device(): jnp.einsum('hrl,hlv->rhv', context, value_up, preferred_element_type=f32)  5.66 us
    unnamed x14, local copies, waits for them, and re-layouts  5.5 us

profile of v3, /device:TPU:0, one launch (start us, length us, event | category | flops | bytes accessed | tf_op | source)
XLA Modules:
  0.0 168.4 jit_solution(2751284329036459521)
XLA Ops:
  0.0 0.8 dynamic-slice_bitcast_fusion.give_ref
  0.8 0.7 broadcast_compare_fusion
  1.5 0.7 broadcast_subtract_fusion
  2.2 0.8 copy.35
  3.0 0.2 select_reduce_fusion.1.limit_ref
  3.2 0.2 fusion.26
  3.4 2.3 %copy-done.1 = bf16[56,64,576]{2,1,0:T(8,128)(2,1)S(1)} copy-done((bf16[56,64,576]{2,1,0:T(8,128)(2,1)S(1)}, bf16[56,64,576]{2,1,0:T(8,128)(2,1)}, u32[]{:S(2)}) %copy-start.1) | copy-done | bytes 4128792
  5.7 1.5 copy-done.2
  7.3 25.8 %shard_map.127 = (bf16[56,32,512]{2,1,0:T(8,128)(2,1)S(1)}, f32[56,1,32]{2,1,0:T(1,128)S(1)}, f32[56,1,32]{2,1,0:T(1,128)S(1)}) custom-call(s32[56]{0:T(128)S(1)} %select_reduce_fusion.2.owner_ref, s32[56]{0:T(128)S(1)} %select_reduce_fusion.1.limit_ref, s32[8]{0:T(128)S(1)} %dynamic-slice_bitcast_fusion.give_ref, bf16[56,64,576]{2,1,0:T(8,128)(2,1)S(1)} %copy-done.1, ...), custom_call_target="tpu_custom_call" | custom-call | tf_op jit(solution)/shard_map/pallas_call | solution.py:128
  33.2 1.2 multiply_reduce_fusion
  34.4 5.7 %fusion.16 = bf16[32,6,8,128]{3,2,1,0:T(8,128)(2,1)S(1)} fusion(bf16[32,512,128]{2,1,0:T(8,128)(2,1)} %param.20, bf16[56,32,512]{2,1,0:T(8,128)(2,1)S(1)} %get-tuple-element.10, f32[32,48,56]{2,1,0:T(8,128)} %get-tuple-element.14, f32[32,48]{1,0:T(8,128)S(1)} %get-tuple-element.13), kind=kOutput, calls=%fused_computation.10 | convolution fusion | flops 290562048 | bytes 6772736 | tf_op jit(solution)/shard_map/hrl,hlv->rhv/dot_general | solution.py:622
  40.2 0.2 constant_dynamic-slice_fusion.stream_ref
  40.4 49.1 %shard_map.128.hidden_ref = bf16[384,448]{1,0:T(8,128)(2,1)S(1)} custom-call(bf16[48,4096]{1,0:T(8,128)(2,1)S(1)} %bitcast.37, bf16[4096,896]{1,0:T(8,128)(2,1)} %w_hbm.1, bf16[384,448]{1,0:T(8,128)(2,1)S(1)} %constant_dynamic-slice_fusion.stream_ref), custom_call_target="tpu_custom_call" | custom-call | tf_op jit(solution)/shard_map/pallas_call | solution.py:298
  89.6 0.7 copy-done.3
  90.4 1.2 reduce-window.6
  91.6 0.2 slice_reduce_fusion
  91.8 0.2 reduce-window.9
  92.0 0.1 add_bitcast_fusion
  92.1 0.1 copy.40
  92.2 0.8 reshape_add_fusion
  93.0 0.6 reshape_add_fusion.1.target_row_ref
  93.6 0.7 reshape.119.gain_ref
  94.3 72.2 %shard_map.129 = bf16[384,448]{1,0:T(8,128)(2,1)} custom-call(bf16[384,448]{1,0:T(8,128)(2,1)} %copy-done.3, s32[1,384]{1,0:T(1,128)} %reshape_add_fusion.1.target_row_ref, s32[384,1]{1,0:T(8,128)} %get-tuple-element.11.target_col_ref, f32[16,1,448]{2,1,0:T(1,128)} %reshape.119.gain_ref, bf16[16,448,256]{2,1,0:T(8,128)(2,1)} %bitcast.40, ...), custom_call_target="tpu_custom_call" | custom-call | tf_op jit(solution)/shard_map/pallas_call | solution.py:534
  166.5 1.9 %copy.43 = bf16[384,448]{0,1:T(8,128)(2,1)} copy(bf16[384,448]{1,0:T(8,128)(2,1)} %shard_map.129) | data formatting | bytes 688128 | tf_op jit(solution)/shard_map/pallas_call | solution.py:534
  (17 shorter events, 0.3 us)
Async XLA Ops:
  0.0 40.2 %copy-start = (bf16[384,896]{1,0:T(8,128)(2,1)S(1)}, bf16[384,896]{1,0:T(8,128)(2,1)}, u32[]{:S(2)}) copy-start(bf16[384,896]{1,0:T(8,128)(2,1)} %param.15) | copy-start | bytes 2064388
  3.4 2.3 %copy-start.1 = (bf16[56,64,576]{2,1,0:T(8,128)(2,1)S(1)}, bf16[56,64,576]{2,1,0:T(8,128)(2,1)}, u32[]{:S(2)}) copy-start(bf16[56,64,576]{2,1,0:T(8,128)(2,1)} %kv_ref.1) | copy-start | bytes 12386308
  5.7 1.5 copy-start.2
  40.4 49.9 %copy-start.5 = (s32[384,1]{0,1:T(1,128)S(1)}, s32[384,1]{0,1:T(1,128)}, u32[]{:S(2)}) copy-start(s32[384,1]{0,1:T(1,128)} %param.19) | copy-start | bytes 4612
  40.4 53.2 %copy-start.4 = (f32[7168]{0:T(1024)S(1)}, f32[7168]{0:T(1024)}, u32[]{:S(2)}) copy-start(f32[7168]{0:T(1024)} %param.22) | copy-start | bytes 86020
  89.6 0.7 copy-start.3

commit v4 on v3

--- a/solution.py
+++ b/solution.py
@@ -40,12 +40,17 @@
 
 
 def attend_kernel(
-    count, each, local, owner_ref, limit_ref, give_ref, kv_ref, q_ref, part_ref, top_ref, mass_ref,
-    out, got, sent_sem, got_sem, pass_sem, passed_sem,
+    count, each, local, owner_ref, limit_ref, give_ref, kv_hbm, q_hbm, part_ref, top_ref, mass_ref,
+    kv_ref, q_ref, load_sem, out, got, sent_sem, got_sem, pass_sem, passed_sem,
 ):
     me = lax.axis_index("afd")
     t = lax.axis_index("tensor")
+    load_kv = pltpu.make_async_copy(kv_hbm, kv_ref, load_sem.at[0])
+    load_q = pltpu.make_async_copy(q_hbm, q_ref, load_sem.at[1])
+    load_kv.start()
+    load_q.start()
     greet([(lax.rem(me + d, count), t) for d in range(1, count)] + [(me, 1 - t)])
+    load_kv.wait()
     latent = part_ref.shape[2]
 
     def page_to(to):
@@ -66,20 +71,28 @@
         got[me, t, j] = kv_ref[give_ref[me * each + j]]
     swap(me, t).start()
 
-    def one(slot, page):
-        scores = lax.dot_general(
-            page, q_ref[owner_ref[slot]], (((1,), (1,)), ((), ())), preferred_element_type=f32
-        ) * score_scale
-        position = lax.broadcasted_iota(jnp.int32, scores.shape, 0)
-        scores = jnp.where(position < limit_ref[slot], scores, -jnp.inf)
-        top = jnp.max(scores, axis=0, keepdims=True)
-        exponent = jnp.exp(scores - top)
-        top_ref[slot] = top
-        mass_ref[slot] = jnp.sum(exponent, axis=0, keepdims=True)
-        part_ref[slot] = lax.dot_general(
-            exponent.astype(bf16), page[:, :latent], (((0,), (0,)), ((), ())),
-            preferred_element_type=f32,
-        ).astype(bf16)
+    def work(items):
+        scores = []
+        for slot, page in items:
+            product = lax.dot_general(
+                page, q_ref[owner_ref[slot]], (((1,), (1,)), ((), ())), preferred_element_type=f32
+            ) * score_scale
+            position = lax.broadcasted_iota(jnp.int32, product.shape, 0)
+            scores.append(jnp.where(position < limit_ref[slot], product, -jnp.inf))
+        tops = [jnp.max(x, axis=0, keepdims=True) for x in scores]
+        exponents = [jnp.exp(x - top) for x, top in zip(scores, tops)]
+        masses = [jnp.sum(x, axis=0, keepdims=True) for x in exponents]
+        parts = [
+            lax.dot_general(
+                x.astype(bf16), page[:, :latent], (((0,), (0,)), ((), ())),
+                preferred_element_type=f32,
+            ).astype(bf16)
+            for x, (slot, page) in zip(exponents, items)
+        ]
+        for (slot, page), top, mass, part in zip(items, tops, masses, parts):
+            top_ref[slot] = top
+            mass_ref[slot] = mass
+            part_ref[slot] = part
 
     def forward(d):
         src = lax.rem(me + d, count)
@@ -89,8 +102,7 @@
     pace = local // count
 
     def resident(i, carry):
-        for j in range(pace):
-            one(i * pace + j, kv_ref[i * pace + j])
+        work([(i * pace + j, kv_ref[i * pace + j]) for j in range(pace)])
         return carry
 
     def resident_and_forward(i, carry):
@@ -98,20 +110,24 @@
         forward(i)
         return carry
 
+    load_q.wait()
     resident(0, 0)
     lax.fori_loop(1, count, resident_and_forward, 0)
     for slot in range(pace * count, local):
-        one(slot, kv_ref[slot])
-
-    def arrived(d, carry):
-        src = lax.rem(me + d, count)
-        swap(src, 1 - t).wait_recv()
-        for side in range(2):
-            for j in range(each):
-                one(local + (src * 2 + side) * each + j, got[src, side, j])
-        return carry
-
-    lax.fori_loop(0, count, arrived, 0)
+        work([(slot, kv_ref[slot])])
+
+    def arrived(i, carry):
+        items = []
+        for d in (2 * i, 2 * i + 1):
+            src = lax.rem(me + d, count)
+            swap(src, 1 - t).wait_recv()
+            for side in range(2):
+                for j in range(each):
+                    items.append((local + (src * 2 + side) * each + j, got[src, side, j]))
+        work(items)
+        return carry
+
+    lax.fori_loop(0, count // 2, arrived, 0)
     for d in range(count):
         to = lax.rem(me + d, count)
         swap(to, t).wait_send()
@@ -125,6 +141,7 @@
     heads = queries.shape[1]
     vmem = pl.BlockSpec(memory_space=pltpu.VMEM)
     smem = pl.BlockSpec(memory_space=pltpu.SMEM)
+    hbm = pl.BlockSpec(memory_space=pl.ANY)
     return pl.pallas_call(
         functools.partial(attend_kernel, count, each, local),
         out_shape=(
@@ -132,9 +149,12 @@
             jax.ShapeDtypeStruct((slots, 1, heads), f32),
             jax.ShapeDtypeStruct((slots, 1, heads), f32),
         ),
-        in_specs=[smem, smem, smem, vmem, vmem],
+        in_specs=[smem, smem, smem, hbm, hbm],
         out_specs=(vmem, vmem, vmem),
         scratch_shapes=[
+            pltpu.VMEM(kv_cache.shape, bf16),
+            pltpu.VMEM(queries.shape, bf16),
+            dma((2,)),
             pltpu.VMEM((count, each, page_len, channels), bf16),
             pltpu.VMEM((count, 2, each, page_len, channels), bf16),
             dma((count,)), dma((count,)), dma((count,)), dma((count,)),
@@ -245,9 +265,10 @@
         acc[...] += jnp.dot(block, w[c * step : (c + 1) * step, :], preferred_element_type=f32)
 
     acc[...] = jnp.zeros_like(acc)
+    begin(0)
     for turn in range(chunks + pairs):
-        if turn < chunks:
-            begin(turn)
+        if turn + 1 < chunks:
+            begin(turn + 1)
         for s in range(pairs - 1, 0, -1):
             if 0 <= turn - s < chunks:
                 relay(turn - s, s)

time: 171 us -> 163 us (0.953)
  Pallas kernels: 147 us -> 139 us
    pallas_call x1, Pallas kernels: 25.8 us -> 20.8 us  [attend(): pl.pallas_call(functools.partial(attend_kernel, count, each, local), out_...]
    pallas_call x1, Pallas kernels: 72.2 us -> 70.4 us  [run_experts(): pl.pallas_call(functools.partial(experts_kernel, pairs), out_shape=jax.Sh...]
    pallas_call x1, Pallas kernels: 49.1 us -> 47.3 us  [project(): pl.pallas_call(functools.partial(project_kernel, pairs), out_shape=jax.Sh...]
where the time goes in v4:
time: 163 us; the launch traced here: 160 us
  Pallas kernels  139 us (85%)
  local copies, waits for them, and re-layouts  9.51 us (6%)
  other arithmetic  6 us (4%)
  matrix products  5.66 us (3%)
    pallas_call x1, Pallas kernels, run_experts(): pl.pallas_call(functools.partial(experts_kernel, pairs), out_shape=jax.Sh...  70.4 us
    pallas_call x1, Pallas kernels, project(): pl.pallas_call(functools.partial(project_kernel, pairs), out_shape=jax.Sh...  47.3 us
    pallas_call x1, Pallas kernels, attend(): pl.pallas_call(functools.partial(attend_kernel, count, each, local), out_...  20.8 us
    dot_general x1, matrix products, on_device(): jnp.einsum('hrl,hlv->rhv', context, value_up, preferred_element_type=f32)  5.66 us
    unnamed x14, local copies, waits for them, and re-layouts  5.5 us

profile of v4, /device:TPU:0, one launch (start us, length us, event | category | flops | bytes accessed | tf_op | source)
XLA Modules:
  0.0 159.8 jit_solution(9155652478108529557)
XLA Ops:
  0.0 0.8 dynamic-slice_bitcast_fusion.give_ref
  0.8 0.7 broadcast_compare_fusion
  1.5 0.7 broadcast_subtract_fusion
  2.2 0.8 copy.35
  3.0 0.2 select_reduce_fusion.1.limit_ref
  3.2 0.2 fusion.26
  3.4 2.3 %copy-done.1 = bf16[56,64,576]{2,1,0:T(8,128)(2,1)S(1)} copy-done((bf16[56,64,576]{2,1,0:T(8,128)(2,1)S(1)}, bf16[56,64,576]{2,1,0:T(8,128)(2,1)}, u32[]{:S(2)}) %copy-start.1) | copy-done | bytes 4128792
  5.7 1.5 copy-done.2
  7.3 20.8 %shard_map.127 = (bf16[56,32,512]{2,1,0:T(8,128)(2,1)S(1)}, f32[56,1,32]{2,1,0:T(1,128)S(1)}, f32[56,1,32]{2,1,0:T(1,128)S(1)}) custom-call(s32[56]{0:T(128)S(1)} %select_reduce_fusion.2.owner_ref, s32[56]{0:T(128)S(1)} %select_reduce_fusion.1.limit_ref, s32[8]{0:T(128)S(1)} %dynamic-slice_bitcast_fusion.give_ref, bf16[56,64,576]{2,1,0:T(8,128)(2,1)S(1)} %copy-done.1, ...), custom_call_target="tpu_custom_call" | custom-call | tf_op jit(solution)/shard_map/pallas_call | solution.py:145
  28.2 1.2 multiply_reduce_fusion
  29.4 5.7 %fusion.16 = bf16[32,6,8,128]{3,2,1,0:T(8,128)(2,1)S(1)} fusion(bf16[32,512,128]{2,1,0:T(8,128)(2,1)} %param.20, bf16[56,32,512]{2,1,0:T(8,128)(2,1)S(1)} %get-tuple-element.10, f32[32,48,56]{2,1,0:T(8,128)} %get-tuple-element.14, f32[32,48]{1,0:T(8,128)S(1)} %get-tuple-element.13), kind=kOutput, calls=%fused_computation.10 | convolution fusion | flops 290562048 | bytes 6772736 | tf_op jit(solution)/shard_map/hrl,hlv->rhv/dot_general | solution.py:643
  35.2 0.2 constant_dynamic-slice_fusion.stream_ref
  35.4 47.3 %shard_map.128.hidden_ref = bf16[384,448]{1,0:T(8,128)(2,1)S(1)} custom-call(bf16[48,4096]{1,0:T(8,128)(2,1)S(1)} %bitcast.37, bf16[4096,896]{1,0:T(8,128)(2,1)} %w_hbm.1, bf16[384,448]{1,0:T(8,128)(2,1)S(1)} %constant_dynamic-slice_fusion.stream_ref), custom_call_target="tpu_custom_call" | custom-call | tf_op jit(solution)/shard_map/pallas_call | solution.py:319
  82.8 0.7 copy-done.3
  83.5 1.2 reduce-window.6
  84.8 0.2 slice_reduce_fusion
  85.0 0.2 reduce-window.9
  85.2 0.1 add_bitcast_fusion
  85.3 0.1 copy.40
  85.4 0.8 reshape_add_fusion
  86.2 0.6 reshape_add_fusion.1.target_row_ref
  86.8 0.7 reshape.119.gain_ref
  87.5 70.4 %shard_map.129 = bf16[384,448]{1,0:T(8,128)(2,1)} custom-call(bf16[384,448]{1,0:T(8,128)(2,1)} %copy-done.3, s32[1,384]{1,0:T(1,128)} %reshape_add_fusion.1.target_row_ref, s32[384,1]{1,0:T(8,128)} %get-tuple-element.11.target_col_ref, f32[16,1,448]{2,1,0:T(1,128)} %reshape.119.gain_ref, bf16[16,448,256]{2,1,0:T(8,128)(2,1)} %bitcast.40, ...), custom_call_target="tpu_custom_call" | custom-call | tf_op jit(solution)/shard_map/pallas_call | solution.py:555
  157.9 1.9 %copy.43 = bf16[384,448]{0,1:T(8,128)(2,1)} copy(bf16[384,448]{1,0:T(8,128)(2,1)} %shard_map.129) | data formatting | bytes 688128 | tf_op jit(solution)/shard_map/pallas_call | solution.py:555
  (17 shorter events, 0.3 us)
Async XLA Ops:
  0.0 35.1 %copy-start = (bf16[384,896]{1,0:T(8,128)(2,1)S(1)}, bf16[384,896]{1,0:T(8,128)(2,1)}, u32[]{:S(2)}) copy-start(bf16[384,896]{1,0:T(8,128)(2,1)} %param.15) | copy-start | bytes 2064388
  3.4 2.3 %copy-start.1 = (bf16[56,64,576]{2,1,0:T(8,128)(2,1)S(1)}, bf16[56,64,576]{2,1,0:T(8,128)(2,1)}, u32[]{:S(2)}) copy-start(bf16[56,64,576]{2,1,0:T(8,128)(2,1)} %kv_hbm.1) | copy-start | bytes 12386308
  5.7 1.5 copy-start.2
  35.4 48.1 %copy-start.5 = (s32[384,1]{0,1:T(1,128)S(1)}, s32[384,1]{0,1:T(1,128)}, u32[]{:S(2)}) copy-start(s32[384,1]{0,1:T(1,128)} %param.19) | copy-start | bytes 4612
  35.4 51.4 %copy-start.4 = (f32[7168]{0:T(1024)S(1)}, f32[7168]{0:T(1024)}, u32[]{:S(2)}) copy-start(f32[7168]{0:T(1024)} %param.22) | copy-start | bytes 86020
  82.8 0.7 copy-start.3
